TPU v7x, 1024 devices: a whole 4x4x32 slice. The times are simulated.
1024 devices in a mesh: owner: 32 (over z), slab: 4 (over y), red: 8 (over x, core).
Axes of the slice: x: 4, y: 4, z: 32, core: 2. Of those that a mesh axis runs over, the one named last changes fastest.
Arguments:
- amplitudes: bfloat16 [2048, 128, 256], P(('owner', 'slab', 'red')), may hold values from -6 to 6
- integrals: bfloat16 [64, 128, 128], P('slab'), may hold values from -0.21875 to 0.21875
- requests: int32 [32, 4, 8, 32], P('owner', 'slab', 'red'), may hold values from 0 to 1
- task_slot: int32 [32, 4, 8, 16, 12], P('owner', 'slab', 'red'), may hold values from 0 to 31
- task_integral: int32 [32, 4, 8, 16, 12], P('owner', 'slab', 'red'), may hold values from 0 to 63
- live_tasks: int32 [32, 4, 8], P('owner', 'slab', 'red'), may hold values from 3 to 12, as said below
- denominators: float32 [2048, 128, 256], P(('owner', 'slab', 'red')), may hold values from 0.5 to 5
Outputs:
- update: float32 [2048, 128, 256], P(('owner', 'slab', 'red'))
Inputs may be any that keep to these rules, and one draw needn't show every extreme that they name: `live_tasks`: slots below a device's count are live; in every draw some devices have all 12 live.
All inputs are finite; a program needn't handle non-finite values.
Results may differ from a plain program's by a relative error of at most 0.0003.
Values may be sent and summed in bfloat16 or wider, within the bound.
No kernel may reach another device: no remote copies, remote signals or barrier semaphores. Data moves between devices by JAX's collectives and lax.ppermute only.
A program may use at most 32 MiB of HBM per device.

v0:
```python
import jax
import jax.numpy as jnp
from jax import lax
from jax.sharding import PartitionSpec as P


def sent_to_all(array, axis):
    length = lax.axis_size(axis)
    return lax.all_to_all(
        jnp.broadcast_to(array[None], (length, *array.shape)), axis, 0, 0, tiled=True
    )


def laid_out(tiles, dim):
    tiles = jnp.moveaxis(tiles, 0, dim)
    shape = tiles.shape
    return tiles.reshape(*shape[:dim], shape[dim] * shape[dim + 1], *shape[dim + 2 :])


def gather_directly(array, axis, dim):
    tiles = sent_to_all(array, axis)
    return laid_out(tiles, dim)


def in_blocks(array, dim, length):
    shape = array.shape
    tiles = array.reshape(*shape[:dim], length, shape[dim] // length, *shape[dim + 1 :])
    return jnp.moveaxis(tiles, dim, 0)


def summed_on_arrival(array, axis, dim):
    length = lax.axis_size(axis)
    tiles = lax.all_to_all(in_blocks(array, dim, length), axis, 0, 0, tiled=True)
    return jnp.sum(tiles, axis=0)


def on_device(amplitudes, integrals, requests, task_slot, task_integral, live_tasks, denominators):
    owners = lax.axis_size("owner")
    per_owner = amplitudes.shape[0]
    wanted = requests.reshape(owners)
    every_tile = lax.all_gather(amplitudes, "owner", axis=0, tiled=True)
    global_index = jnp.arange(owners, dtype=jnp.int32) * per_owner + wanted
    pulled = jnp.take(every_tile, global_index, axis=0)
    gathered_integrals = gather_directly(integrals, "slab", 0)
    group_tiles = task_slot.shape[3]
    slot_count = task_slot.shape[4]
    slot_table = task_slot.reshape(group_tiles, slot_count)
    integral_table = task_integral.reshape(group_tiles, slot_count)
    live_count = live_tasks.reshape(())
    slot_width = 4
    tile_rows = amplitudes.shape[1]
    tile_columns = amplitudes.shape[2]

    def accumulate(block_index, partial_value):
        first_slot = block_index * slot_width
        slot_block = lax.dynamic_slice_in_dim(slot_table, first_slot, slot_width, 1)
        integral_block = lax.dynamic_slice_in_dim(integral_table, first_slot, slot_width, 1)
        live_mask = (first_slot + jnp.arange(slot_width, dtype=jnp.int32) < live_count).astype(
            jnp.bfloat16
        )
        integral_rows = (
            jnp.take(gathered_integrals, integral_block, axis=0) * live_mask[None, :, None, None]
        )
        amplitude_rows = jnp.take(pulled, slot_block, axis=0)
        return partial_value + jnp.einsum(
            "qkac,qkcx->qax", integral_rows, amplitude_rows, preferred_element_type=jnp.float32
        )

    blocks_live = (live_count + slot_width - 1) // slot_width
    initial = jnp.zeros((group_tiles, tile_rows, tile_columns), jnp.float32)
    partial_value = lax.fori_loop(0, blocks_live, accumulate, initial)
    residual = summed_on_arrival(partial_value, "red", 0)
    return residual / denominators


def solution(mesh):
    placed = (
        P(("owner", "slab", "red"), None, None),
        P("slab", None, None),
        P("owner", "slab", "red", None),
        P("owner", "slab", "red", None, None),
        P("owner", "slab", "red", None, None),
        P("owner", "slab", "red"),
        P(("owner", "slab", "red"), None, None),
    )
    return jax.shard_map(
        on_device,
        mesh=mesh,
        in_specs=placed,
        out_specs=P(("owner", "slab", "red"), None, None),
        check_vma=False,
    )
```

profile of v0, /device:TPU:104, one launch (start us, length us, event | category | flops | bytes accessed | tf_op | source)
XLA Modules:
  0.0 244.7 jit_solution(17313827812975473884)
XLA Ops:
  6.5 0.0 all-gather.2.cloned.1.call-start
  6.5 0.7 all-gather.2.cloned.1.call-update
  7.3 2.9 %broadcast_in_dim.45 = bf16[4,16,128,128]{3,2,1,0:T(8,128)(2,1)} broadcast(bf16[16,128,128]{2,1,0:T(8,128)(2,1)} %param.10), dimensions={1,2,3} | broadcast | bytes 2621440 | tf_op jit(solution)/shard_map/broadcast_in_dim | solution.py:10
  10.2 0.0 copy-start.1
  10.2 0.0 copy-start.2
  10.2 0.0 copy-start.3
  10.2 5.0 %all-to-all-start = ((bf16[4,16,128,128]{3,2,1,0:T(8,128)(2,1)}), bf16[4,16,128,128]{3,2,1,0:T(8,128)(2,1)}, u32[]{:S(2)}, u32[]{:S(2)}) async-start(bf16[4,16,128,128]{3,2,1,0:T(8,128)(2,1)} %broadcast_in_dim.45), calls=%async_computation | async-start | bytes 4194304 | tf_op jit(solution)/shard_map/all_to_all | solution.py:9
  15.9 0.0 copy-done.1
  15.9 0.1 copy.13
  16.0 0.0 copy-done.2
  16.0 0.1 copy.12
  16.1 0.0 copy-done.3
  16.1 142.2 %all-gather.2.cloned.1.call-done = bf16[64,128,256]{2,1,0:T(8,128)(2,1)} async-done(((bf16[2,128,256]{2,1,0:T(8,128)(2,1)}), bf16[64,128,256]{2,1,0:T(8,128)(2,1)}) %all-gather.2.cloned.1.call-update) | async-done | bytes 4194320 | tf_op jit(solution)/shard_map/all_gather | solution.py:41
  158.3 4.2 %gather_fusion.2 = bf16[32,128,256]{2,1,0:T(8,128)(2,1)} fusion(bf16[64,128,256]{2,1,0:T(8,128)(2,1)} %all-gather.2.cloned.1.call-done, s32[1024]{0:T(1024)S(1)} %pad_clamp_fusion.2), kind=kCustom, calls=%fused_computation.2 | custom fusion | bytes 4194432 | tf_op jit(solution)/shard_map/jit(_take)/gather | solution.py:43
  162.6 1.8 broadcast_select_fusion
  164.4 0.0 all-to-all-done
  164.4 1.6 broadcast_in_dim.44
  166.0 13.3 %while.10 = (s32[]{:T(128)}, f32[16,128,256]{2,1,0:T(8,128)}, s32[]{:T(128)}, s32[16,12]{1,0:T(8,128)S(1)}, bf16[64,128,128]{2,1,0:T(8,128)(2,1)}, /*index=5*/s3...) while((s32[]{:T(128)}, f32[16,128,256]{2,1,0:T(8,128)}, ...), condition=%wide.region_1.2_spmd, body=%wide.region_0.1_spmd.sunk | while | flops 541592320 | bytes 23080384 | solution.py:71
  166.0 0.6 compare_convert_fusion.2
  166.7 0.1 compare_and_fusion.4
  166.7 0.1 reshape.116
  166.8 0.1 reshape.117
  167.0 3.8 %gather_fusion.1 = bf16[64,128,128]{2,1,0:T(8,128)(2,1)} fusion(bf16[64,128,128]{2,1,0:T(8,128)(2,1)} %get-tuple-element.157, s32[1024]{0:T(1024)S(1)} %pad_clamp_fusion.6), kind=kCustom, calls=%fused_computation.clone.1 | custom fusion | bytes 4194560 | tf_op jit(solution)/shard_map/while/body/jit(_take)/gather | solution.py:62
  170.7 2.7 %gather_fusion = bf16[64,128,256]{2,1,0:T(8,128)(2,1)} fusion(bf16[32,128,256]{2,1,0:T(8,128)(2,1)S(1)} %get-tuple-element.160, s32[1024]{0:T(1024)S(1)} %pad_clamp_fusion.5), kind=kCustom, calls=%fused_computation.1.clone.1 | custom fusion | bytes 8388864 | tf_op jit(solution)/shard_map/while/body/jit(_take)/gather | solution.py:64
  173.5 5.9 %bitcast_add_fusion.4 = f32[16,128,256]{2,1,0:T(8,128)} fusion(f32[16,128,256]{2,1,0:T(8,128)} %get-tuple-element.142, bf16[16,4,128,256]{3,2,1,0:T(8,128)(2,1)} %bitcast.27, pred[16,4]{1,0:T(8,128)(4,1)S(1)} %get-tuple-element.126, bf16[16,4,128,128]{3,2,1,0:T(8,128)(2,1)} %bitcast.28, pred[16,4]{1,0:T(8,128)(4,1)S(1)} %get-tuple-element.128, ...), kind=kOutput, calls=%fused_computation.6.clone.1 | convolution fusion | flops 541589504 | bytes 10485896 | tf_op jit(solution)/shard_map/while/body/qkac,qkcx->qax/dot_general | solution.py:65
  179.3 56.9 %all_to_all.10 = f32[8,2,128,256]{3,2,1,0:T(8,128)S(1)} all-to-all(f32[8,2,128,256]{3,2,1,0:T(8,128)} %bitcast.29), channel_id=1, replica_groups=mesh['owner'=32,'slab'=4,'red'=8] {'red'}, dimensions={0} | all-to-all | bytes 4194304 | tf_op jit(solution)/shard_map/all_to_all | solution.py:33
  236.2 0.0 copy-start
  236.2 0.1 reduce_sum.9
  236.4 0.8 copy-done
  237.2 0.7 div.14
  (5 shorter events, 0.0 us)
Async XLA Ops:
  6.5 151.8 %all-gather.2.cloned.1.call-start = ((), (), s32[]{:S(2)}) async-start(), calls=%async_computation.2 | async-start | bytes 4325376 | tf_op jit(solution)/shard_map/all_gather | solution.py:41
  10.2 5.7 %copy-start.1 = (s32[1,1,1,16,12]{3,2,4,1,0:T(1,128)S(1)}, s32[1,1,1,16,12]{3,2,4,1,0:T(1,128)}, u32[]{:S(2)}) copy-start(s32[1,1,1,16,12]{3,2,4,1,0:T(1,128)} %param.12) | copy-start | bytes 2308
  10.2 5.8 %copy-start.2 = (s32[1,1,1,16,12]{3,2,4,1,0:T(1,128)S(1)}, s32[1,1,1,16,12]{3,2,4,1,0:T(1,128)}, u32[]{:S(2)}) copy-start(s32[1,1,1,16,12]{3,2,4,1,0:T(1,128)} %param.13) | copy-start | bytes 2308
  10.2 5.9 %copy-start.3 = (s32[1,1,1,32]{3,2,1,0:T(1,128)S(1)}, s32[1,1,1,32]{3,2,1,0:T(1,128)}, u32[]{:S(2)}) copy-start(s32[1,1,1,32]{3,2,1,0:T(1,128)} %param.11) | copy-start | bytes 388
  10.2 154.2 %all-to-all-start = ((bf16[4,16,128,128]{3,2,1,0:T(8,128)(2,1)}), bf16[4,16,128,128]{3,2,1,0:T(8,128)(2,1)}, u32[]{:S(2)}, u32[]{:S(2)}) async-start(bf16[4,16,128,128]{3,2,1,0:T(8,128)(2,1)} %broadcast_in_dim.45), calls=%async_computation | async-start | bytes 4194304 | tf_op jit(solution)/shard_map/all_to_all | solution.py:9
  236.2 1.0 copy-start
Sparse Core Ops, SparseCore 0:
  10.0 148.2 all-gather.1
where the time goes:
time: 248 us; the launch traced here: 245 us
  waiting for transfers between devices  143 us (58%)
  blocking collectives  56.9 us (23%)
  local copies, waits for them, and re-layouts  16.4 us (7%)
  between operations  14.1 us (6%)
  matrix products  5.86 us (2%)
  starting transfers between devices  5.04 us (2%)
  other arithmetic  3.5 us (1%)
    all_gather x1, waiting for transfers between devices, on_device(): every_tile = lax.all_gather(amplitudes, 'owner', axis=0, tiled=True)  142 us
    all_to_all x1, blocking collectives, summed_on_arrival(): lax.all_to_all(in_blocks(array, dim, length), axis, 0, 0, tiled=True)  56.9 us
    dot_general x1, matrix products, accumulate(): jnp.einsum('qkac,qkcx->qax', integral_rows, amplitude_rows, preferred_ele...  5.86 us
    all_to_all x1, starting transfers between devices, sent_to_all(): lax.all_to_all(jnp.broadcast_to(array[None], (length, *array.shape)), axi...  5.04 us
  transfers between devices with their start and end apart: 2, of which 1 were waited for; matrix products, arithmetic and copies ran while one was open for 4% of the time, Pallas kernels for 0%

commit v1 on v0

v1 whole, which is shorter than its diff:
```python
import functools

import jax
import jax.numpy as jnp
from jax import lax
from jax.experimental import pallas as pl
from jax.experimental.pallas import tpu as pltpu
from jax.sharding import PartitionSpec as P

VMEM = pltpu.VMEM
SMEM = pltpu.SMEM
LIFT = 2.0**13
WIDTH = 4


def contract(per_chip, flip, place, live, slots, ints, integrals, pulled, out):
    tiles = out.shape[0]
    slot_count = slots.shape[1]
    half = lax.bitwise_xor(lax.rem(place[0], 2), flip)
    live_count = live[0]
    groups = lax.div(live_count + (WIDTH - 1), WIDTH)

    def tile(t, _):
        q = lax.div(t, per_chip) * (2 * per_chip) + half * per_chip + lax.rem(t, per_chip)

        def some(g):
            left, right = [], []
            for w in range(WIDTH):
                k = jnp.minimum(g * WIDTH + w, slot_count - 1)
                alive = g * WIDTH + w < live_count
                block = integrals[ints[q, k]]
                left.append(jnp.where(alive, block, jnp.zeros_like(block)))
                right.append(pulled[slots[q, k]])
            return jnp.dot(
                jnp.concatenate(left, axis=1),
                jnp.concatenate(right, axis=0),
                preferred_element_type=jnp.float32,
            )

        out[t] = some(0)

        def more(g, _):
            out[t] += some(g)
            return 0

        lax.fori_loop(1, groups, more, 0)
        return 0

    lax.fori_loop(0, tiles, tile, 0)


def call_contract(flip, per_chip, tiles, place, live, slots, ints, integrals, pulled):
    rows, columns = integrals.shape[1], pulled.shape[2]
    return pl.pallas_call(
        functools.partial(contract, per_chip, flip),
        out_shape=jax.ShapeDtypeStruct((tiles, rows, columns), jnp.float32),
        in_specs=[pl.BlockSpec(memory_space=SMEM)] * 4 + [pl.BlockSpec(memory_space=VMEM)] * 2,
        out_specs=pl.BlockSpec(memory_space=VMEM),
        compiler_params=pltpu.CompilerParams(vmem_limit_bytes=32 * 2**20),
        cost_estimate=pl.CostEstimate(
            flops=2 * tiles * 12 * rows * rows * columns,
            bytes_accessed=4 * tiles * rows * columns,
            transcendentals=0,
        ),
    )(place, live, slots, ints, integrals, pulled)


def combine(per_chip, place, mine, came, own, *sends):
    chips = len(sends) + 1
    here = lax.div(place[0], 2)
    for d in range(chips):
        first = lax.rem(here + d, chips) * per_chip
        target = own if d == 0 else sends[d - 1]
        for j in range(per_chip):
            target[j] = mine[first + j] + came[first + j]


def call_combine(per_chip, chips, place, mine, came):
    shape = jax.ShapeDtypeStruct((per_chip, *mine.shape[1:]), jnp.float32)
    return pl.pallas_call(
        functools.partial(combine, per_chip),
        out_shape=(shape,) * chips,
        in_specs=[pl.BlockSpec(memory_space=SMEM)] + [pl.BlockSpec(memory_space=VMEM)] * 2,
        out_specs=(pl.BlockSpec(memory_space=VMEM),) * chips,
        compiler_params=pltpu.CompilerParams(vmem_limit_bytes=32 * 2**20),
    )(place, mine, came)


def on_device(amplitudes, integrals, requests, task_slot, task_integral, live_tasks, denominators):
    owners = lax.axis_size("owner")
    reds = lax.axis_size("red")
    chips = reds // 2
    group_tiles, slot_count = task_slot.shape[3:]
    per_chip = group_tiles // reds
    tiles = group_tiles // 2
    wanted = requests.reshape(owners)
    slots = task_slot.reshape(group_tiles, slot_count)
    ints = task_integral.reshape(group_tiles, slot_count)
    live = live_tasks.reshape(1)
    place = lax.axis_index("red").reshape(1).astype(jnp.int32)

    every_integral = lax.all_gather(integrals, "slab", axis=0, tiled=True)
    lifted = (amplitudes * jnp.asarray(LIFT, amplitudes.dtype)).astype(jnp.float16)
    every = lax.all_gather(lifted, "owner", axis=0, tiled=True)
    every = every.reshape(owners, -1, *every.shape[1:])
    pulled = jnp.where((wanted == 0)[:, None, None], every[:, 0], every[:, 1])
    pulled = (pulled.astype(jnp.float32) * (1 / LIFT)).astype(jnp.bfloat16)

    tables = (place, live, slots, ints, every_integral, pulled)
    other = call_contract(1, per_chip, tiles, *tables)
    came = lax.ppermute(other, "red", [(k, k ^ 1) for k in range(reds)])
    mine = call_contract(0, per_chip, tiles, *tables)
    own, *sends = call_combine(per_chip, chips, place, mine, came)
    total = own
    for d, send in enumerate(sends, 1):
        total = total + lax.ppermute(send, "red", [(k, (k + 2 * d) % reds) for k in range(reds)])
    return total / denominators


def solution(mesh):
    placed = (
        P(("owner", "slab", "red"), None, None),
        P("slab", None, None),
        P("owner", "slab", "red", None),
        P("owner", "slab", "red", None, None),
        P("owner", "slab", "red", None, None),
        P("owner", "slab", "red"),
        P(("owner", "slab", "red"), None, None),
    )
    return jax.shard_map(
        on_device,
        mesh=mesh,
        in_specs=placed,
        out_specs=P(("owner", "slab", "red"), None, None),
        check_vma=False,
    )
```

time: 248 us -> 149 us (0.60)
  the two profiles are of different devices: /device:TPU:104 before, /device:TPU:6 now
where the time goes in v1:
time: 149 us; the launch traced here: 146 us
  blocking collectives  95.6 us (64%)
  between operations  14.1 us (9%)
  starting transfers between devices  13.6 us (9%)
  waiting for transfers between devices  11.3 us (8%)
  Pallas kernels  4.94 us (3%)
  other arithmetic  3.71 us (2%)
  local copies, waits for them, and re-layouts  3.12 us (2%)
    all_gather x1, blocking collectives, on_device(): every = lax.all_gather(lifted, 'owner', axis=0, tiled=True)  95.6 us
    ppermute x3, starting transfers between devices, on_device(): lax.ppermute(send, 'red', [(k, (k + 2 * d) % reds) for k in range(reds)])  11.6 us
    ppermute x3, waiting for transfers between devices, on_device(): lax.ppermute(send, 'red', [(k, (k + 2 * d) % reds) for k in range(reds)])  10.4 us
    pallas_call x2, Pallas kernels, call_contract(): pl.pallas_call(functools.partial(contract, per_chip, flip), out_shape=jax...  4.83 us
    unnamed x6, local copies, waits for them, and re-layouts  3.12 us
  transfers between devices with their start and end apart: 5, of which 4 were waited for; matrix products, arithmetic and copies ran while one was open for 3% of the time, Pallas kernels for 2%

profile of v1, /device:TPU:6, one launch (start us, length us, event | category | flops | bytes accessed | tf_op | source)
XLA Modules:
  0.0 146.4 jit_solution(1763767143027401380)
XLA Ops:
  6.5 0.0 all-gather.3.cloned.1.call-start
  6.5 0.7 all-gather.3.cloned.1.call-update
  7.3 0.8 copy.14
  8.0 0.8 copy.15
  9.4 0.7 compare_bitcast_fusion
  10.1 0.9 multiply_convert_fusion.1
  11.0 95.6 %all-gather.4 = f16[64,128,256]{2,1,0:T(8,128)(2,1)S(1)} all-gather(f16[2,128,256]{2,1,0:T(8,128)(2,1)S(1)} %multiply_convert_fusion.1), channel_id=1, replica_groups=mesh['owner'=32,'slab'=4,'red'=8] {'owner'}, dimensions={0}, use_global_device_ids=true | all-gather | bytes 4325376 | tf_op jit(solution)/shard_map/all_gather | solution.py:104
  106.6 1.3 multiply_convert_fusion.pulled
  108.0 0.0 all-gather.3.cloned.1.call-done.integrals
  108.0 0.0 copy-start
  108.0 1.6 %copy-done = bf16[64,128,128]{2,1,0:T(8,128)(2,1)S(1)} copy-done((bf16[64,128,128]{2,1,0:T(8,128)(2,1)S(1)}, bf16[64,128,128]{2,1,0:T(8,128)(2,1)}, u32[]{:S(2)}) %copy-start) | copy-done | bytes 2097176
  109.6 2.4 %shard_map.74 = f32[8,128,256]{2,1,0:T(8,128)S(1)} custom-call(s32[1]{0:T(128)} %bitcast.place, s32[1]{0:T(128)} %bitcast.22.live, s32[16,12]{1,0:T(8,128)S(1)} %bitcast.23, s32[16,12]{1,0:T(8,128)S(1)} %bitcast.25, bf16[64,128,128]{2,1,0:T(8,128)(2,1)S(1)} %copy-done, bf16[32,128,256]{2,1,0:T(8,128)(2,1)S(1)} %multiply_convert_fusion.pulled), custom_call_target="tpu_custom_call" | custom-call | flops 805306368 | bytes 1048576 | tf_op jit(solution)/shard_map/pallas_call | solution.py:54
  112.0 1.9 %collective-permute-start = (f32[8,128,256]{2,1,0:T(8,128)S(1)}, f32[8,128,256]{2,1,0:T(8,128)S(1)}, u32[]{:S(2)}, u32[]{:S(2)}) collective-permute-start(f32[8,128,256]{2,1,0:T(8,128)S(1)} %shard_map.74), channel_id=1, source_target_pairs={{0,1},{1,0},{2,3},{3,2},{4,5},{5,4},{6,7},{7,6},{8,9},{9,8},{10,11... | collective-permute-start | bytes 3145736 | tf_op jit(solution)/shard_map/ppermute | solution.py:111
  114.0 2.4 %shard_map.73.mine = f32[8,128,256]{2,1,0:T(8,128)S(1)} custom-call(s32[1]{0:T(128)} %bitcast.place, s32[1]{0:T(128)} %bitcast.21.live, s32[16,12]{1,0:T(8,128)S(1)} %bitcast.24, s32[16,12]{1,0:T(8,128)S(1)} %bitcast.26, bf16[64,128,128]{2,1,0:T(8,128)(2,1)S(1)} %copy-done, bf16[32,128,256]{2,1,0:T(8,128)(2,1)S(1)} %multiply_convert_fusion.pulled), custom_call_target="tpu_custom_call" | custom-call | flops 805306368 | bytes 1048576 | tf_op jit(solution)/shard_map/pallas_call | solution.py:54
  116.4 0.0 copy-start.1
  116.4 0.2 collective-permute-done.came
  116.6 0.1 shard_map.75
  116.7 2.4 %collective-permute-start.1 = (f32[2,128,256]{2,1,0:T(8,128)S(1)}, f32[2,128,256]{2,1,0:T(8,128)S(1)}, u32[]{:S(2)}, u32[]{:S(2)}) collective-permute-start(f32[2,128,256]{2,1,0:T(8,128)S(1)} %get-tuple-element.10), channel_id=1, source_target_pairs={{0,2},{1,3},{2,4},{3,5},{4,6},{5,7},{6,0},{7,1},{8,10},{9,11},{10,... | collective-permute-start | bytes 786440 | tf_op jit(solution)/shard_map/ppermute | solution.py:116
  119.1 7.3 %collective-permute-start.2 = (f32[2,128,256]{2,1,0:T(8,128)S(1)}, f32[2,128,256]{2,1,0:T(8,128)S(1)}, u32[]{:S(2)}, u32[]{:S(2)}) collective-permute-start(f32[2,128,256]{2,1,0:T(8,128)S(1)} %get-tuple-element.11), channel_id=1, source_target_pairs={{0,4},{1,5},{2,6},{3,7},{4,0},{5,1},{6,2},{7,3},{8,12},{9,13},{10,... | collective-permute-start | bytes 786440 | tf_op jit(solution)/shard_map/ppermute | solution.py:116
  126.4 1.9 %collective-permute-start.3 = (f32[2,128,256]{2,1,0:T(8,128)S(1)}, f32[2,128,256]{2,1,0:T(8,128)S(1)}, u32[]{:S(2)}, u32[]{:S(2)}) collective-permute-start(f32[2,128,256]{2,1,0:T(8,128)S(1)} %get-tuple-element.12), channel_id=1, source_target_pairs={{0,6},{1,7},{2,0},{3,1},{4,2},{5,3},{6,4},{7,5},{8,14},{9,15},{10,... | collective-permute-start | bytes 786440 | tf_op jit(solution)/shard_map/ppermute | solution.py:116
  128.4 1.2 collective-permute-done.1
  129.6 3.9 %collective-permute-done.2 = f32[2,128,256]{2,1,0:T(8,128)S(1)} collective-permute-done((f32[2,128,256]{2,1,0:T(8,128)S(1)}, f32[2,128,256]{2,1,0:T(8,128)S(1)}, u32[]{:S(2)}, u32[]{:S(2)}) %collective-permute-start.2) | collective-permute-done | bytes 262176 | tf_op jit(solution)/shard_map/ppermute | solution.py:116
  133.5 5.2 %collective-permute-done.3 = f32[2,128,256]{2,1,0:T(8,128)S(1)} collective-permute-done((f32[2,128,256]{2,1,0:T(8,128)S(1)}, f32[2,128,256]{2,1,0:T(8,128)S(1)}, u32[]{:S(2)}, u32[]{:S(2)}) %collective-permute-start.3) | collective-permute-done | bytes 262176 | tf_op jit(solution)/shard_map/ppermute | solution.py:116
  138.7 0.0 copy-done.1
  138.7 0.8 add_divide_fusion
Async XLA Ops:
  6.5 101.5 %all-gather.3.cloned.1.call-start = ((), (), s32[]{:S(2)}) async-start(), calls=%async_computation | async-start | bytes 2621440 | tf_op jit(solution)/shard_map/all_gather | solution.py:102
  108.0 1.6 %copy-start = (bf16[64,128,128]{2,1,0:T(8,128)(2,1)S(1)}, bf16[64,128,128]{2,1,0:T(8,128)(2,1)}, u32[]{:S(2)}) copy-start(bf16[64,128,128]{2,1,0:T(8,128)(2,1)} %all-gather.3.cloned.1.call-done.integrals) | copy-start | bytes 6291460
  112.0 4.6 %collective-permute-start = (f32[8,128,256]{2,1,0:T(8,128)S(1)}, f32[8,128,256]{2,1,0:T(8,128)S(1)}, u32[]{:S(2)}, u32[]{:S(2)}) collective-permute-start(f32[8,128,256]{2,1,0:T(8,128)S(1)} %shard_map.74), channel_id=1, source_target_pairs={{0,1},{1,0},{2,3},{3,2},{4,5},{5,4},{6,7},{7,6},{8,9},{9,8},{10,11... | collective-permute-start | bytes 3145736 | tf_op jit(solution)/shard_map/ppermute | solution.py:111
  116.4 22.3 %copy-start.1 = (f32[2,128,256]{2,1,0:T(8,128)S(1)}, f32[2,128,256]{2,1,0:T(8,128)}, u32[]{:S(2)}) copy-start(f32[2,128,256]{2,1,0:T(8,128)} %param.13) | copy-start | bytes 786436
  116.7 12.9 %collective-permute-start.1 = (f32[2,128,256]{2,1,0:T(8,128)S(1)}, f32[2,128,256]{2,1,0:T(8,128)S(1)}, u32[]{:S(2)}, u32[]{:S(2)}) collective-permute-start(f32[2,128,256]{2,1,0:T(8,128)S(1)} %get-tuple-element.10), channel_id=1, source_target_pairs={{0,2},{1,3},{2,4},{3,5},{4,6},{5,7},{6,0},{7,1},{8,10},{9,11},{10,... | collective-permute-start | bytes 786440 | tf_op jit(solution)/shard_map/ppermute | solution.py:116
  119.1 14.4 %collective-permute-start.2 = (f32[2,128,256]{2,1,0:T(8,128)S(1)}, f32[2,128,256]{2,1,0:T(8,128)S(1)}, u32[]{:S(2)}, u32[]{:S(2)}) collective-permute-start(f32[2,128,256]{2,1,0:T(8,128)S(1)} %get-tuple-element.11), channel_id=1, source_target_pairs={{0,4},{1,5},{2,6},{3,7},{4,0},{5,1},{6,2},{7,3},{8,12},{9,13},{10,... | collective-permute-start | bytes 786440 | tf_op jit(solution)/shard_map/ppermute | solution.py:116
  126.4 12.3 %collective-permute-start.3 = (f32[2,128,256]{2,1,0:T(8,128)S(1)}, f32[2,128,256]{2,1,0:T(8,128)S(1)}, u32[]{:S(2)}, u32[]{:S(2)}) collective-permute-start(f32[2,128,256]{2,1,0:T(8,128)S(1)} %get-tuple-element.12), channel_id=1, source_target_pairs={{0,6},{1,7},{2,0},{3,1},{4,2},{5,3},{6,4},{7,5},{8,14},{9,15},{10,... | collective-permute-start | bytes 786440 | tf_op jit(solution)/shard_map/ppermute | solution.py:116
Sparse Core Ops, SparseCore 0:
  10.0 56.1 all-gather.2

commit v2 on v1

v2 whole, which is shorter than its diff:
```python
import functools

import jax
import jax.numpy as jnp
from jax import lax
from jax.experimental import pallas as pl
from jax.experimental.pallas import tpu as pltpu
from jax.sharding import PartitionSpec as P

VMEM = pltpu.VMEM
SMEM = pltpu.SMEM
LIFT = 2.0**13
WIDTH = 4


def place_here():
    return lax.axis_index("red").astype(jnp.int32)


def contract(per_chip, flip, live, slots, ints, integrals, pulled, out):
    tiles = out.shape[0]
    slot_count = slots.shape[2]
    live_count = live[0, 0, 0]
    half = lax.bitwise_xor(lax.rem(place_here(), 2), flip)
    groups = lax.div(live_count + (WIDTH - 1), WIDTH)

    def tile(t, _):
        q = lax.div(t, per_chip) * (2 * per_chip) + half * per_chip + lax.rem(t, per_chip)

        def some(g):
            left, right = [], []
            for w in range(WIDTH):
                k = jnp.minimum(g * WIDTH + w, slot_count - 1)
                alive = g * WIDTH + w < live_count
                block = integrals[ints[0, 0, k, 0, q]]
                left.append(jnp.where(alive, block, jnp.zeros_like(block)))
                right.append(pulled[slots[0, 0, k, 0, q]])
            return jnp.dot(
                jnp.concatenate(left, axis=1),
                jnp.concatenate(right, axis=0),
                preferred_element_type=jnp.float32,
            )

        out[t] = some(0)

        def more(g, _):
            out[t] += some(g)
            return 0

        lax.fori_loop(1, groups, more, 0)
        return 0

    lax.fori_loop(0, tiles, tile, 0)


def call_contract(flip, per_chip, tiles, live, slots, ints, integrals, pulled):
    rows, columns = integrals.shape[1], pulled.shape[2]
    return pl.pallas_call(
        functools.partial(contract, per_chip, flip),
        out_shape=jax.ShapeDtypeStruct((tiles, rows, columns), jnp.float32),
        in_specs=[pl.BlockSpec(memory_space=SMEM)] * 3 + [pl.BlockSpec(memory_space=VMEM)] * 2,
        out_specs=pl.BlockSpec(memory_space=VMEM),
        compiler_params=pltpu.CompilerParams(vmem_limit_bytes=32 * 2**20),
        cost_estimate=pl.CostEstimate(
            flops=2 * tiles * 12 * rows * rows * columns,
            bytes_accessed=4 * tiles * rows * columns,
            transcendentals=0,
        ),
    )(live, slots, ints, integrals, pulled)


def partner(chip, core, step):
    return chip ^ 1 if (core + step) % 2 == 0 else 3 - chip


def combine(per_chip, mine, came, keep, send):
    place = place_here()
    here, core = lax.div(place, 2), lax.rem(place, 2)
    near = lax.bitwise_xor(here, 1)
    first = jnp.where(core == 0, near, 3 - here)
    second = jnp.where(core == 0, 3 - here, near)
    across = lax.bitwise_xor(here, 2)
    for block, target, at in ((first, send, 0), (across, send, 1), (here, keep, 0), (second, keep, 1)):
        for j in range(per_chip):
            t = block * per_chip + j
            target[at, j] = mine[t] + came[t]


def call_combine(per_chip, mine, came):
    shape = jax.ShapeDtypeStruct((2, per_chip, *mine.shape[1:]), jnp.float32)
    return pl.pallas_call(
        functools.partial(combine, per_chip),
        out_shape=(shape, shape),
        in_specs=[pl.BlockSpec(memory_space=VMEM)] * 2,
        out_specs=(pl.BlockSpec(memory_space=VMEM),) * 2,
        compiler_params=pltpu.CompilerParams(vmem_limit_bytes=32 * 2**20),
    )(mine, came)


def on_device(amplitudes, integrals, requests, task_slot, task_integral, live_tasks, denominators):
    owners = lax.axis_size("owner")
    reds = lax.axis_size("red")
    group_tiles = task_slot.shape[3]
    per_chip = group_tiles // reds
    tiles = group_tiles // 2
    wanted = requests.reshape(owners)
    slots, ints = (jnp.transpose(t, (0, 1, 4, 2, 3)) for t in (task_slot, task_integral))

    every_integral = lax.all_gather(integrals, "slab", axis=0, tiled=True)
    lifted = (amplitudes * jnp.asarray(LIFT, amplitudes.dtype)).astype(jnp.float16)
    every = lax.all_gather(lifted, "owner", axis=0, tiled=True)
    every = every.reshape(owners, -1, *every.shape[1:])
    pulled = jnp.where((wanted == 0)[:, None, None], every[:, 0], every[:, 1])
    pulled = (pulled.astype(jnp.float32) * (1 / LIFT)).astype(jnp.bfloat16)

    tables = (live_tasks, slots, ints, every_integral, pulled)
    other = call_contract(1, per_chip, tiles, *tables)
    came = lax.ppermute(other, "red", [(k, k ^ 1) for k in range(reds)])
    mine = call_contract(0, per_chip, tiles, *tables)
    keep, send = call_combine(per_chip, mine, came)
    ways = [[(k, 2 * partner(k // 2, k % 2, step) + k % 2) for k in range(reds)] for step in range(2)]
    half = lax.ppermute(send, "red", ways[0])
    last = lax.ppermute(keep[1] + half[1], "red", ways[1])
    return (keep[0] + half[0] + last) / denominators


def solution(mesh):
    placed = (
        P(("owner", "slab", "red"), None, None),
        P("slab", None, None),
        P("owner", "slab", "red", None),
        P("owner", "slab", "red", None, None),
        P("owner", "slab", "red", None, None),
        P("owner", "slab", "red"),
        P(("owner", "slab", "red"), None, None),
    )
    return jax.shard_map(
        on_device,
        mesh=mesh,
        in_specs=placed,
        out_specs=P(("owner", "slab", "red"), None, None),
        check_vma=False,
    )
```

time: 149 us -> 150 us (level)
  the two profiles are of different devices: /device:TPU:6 before, /device:TPU:8 now
where the time goes in v2:
time: 150 us
  blocking collectives  96.8 us (65%)
  waiting for transfers between devices  15.7 us (10%)
  between operations  14.1 us (9%)
  starting transfers between devices  13.3 us (9%)
  Pallas kernels  4.83 us (3%)
  other arithmetic  3.74 us (2%)
  local copies, waits for them, and re-layouts  1.6 us (1%)
    all_gather x1, blocking collectives, on_device(): every = lax.all_gather(lifted, 'owner', axis=0, tiled=True)  96.8 us
    ppermute x1, starting transfers between devices, on_device(): half = lax.ppermute(send, 'red', ways[0])  9.44 us
    ppermute x1, waiting for transfers between devices, on_device(): last = lax.ppermute(keep[1] + half[1], 'red', ways[1])  7.55 us
    ppermute x1, waiting for transfers between devices, on_device(): half = lax.ppermute(send, 'red', ways[0])  7.14 us
    pallas_call x2, Pallas kernels, call_contract(): pl.pallas_call(functools.partial(contract, per_chip, flip), out_shape=jax...  4.72 us
  transfers between devices with their start and end apart: 4, of which 3 were waited for; matrix products, arithmetic and copies ran while one was open for 2% of the time, Pallas kernels for 2%

profile of v2, /device:TPU:8, one launch (start us, length us, event | category | flops | bytes accessed | tf_op | source)
XLA Modules:
  0.0 150.1 jit_solution(8072356405421020829)
XLA Ops:
  6.5 0.0 all-gather.3.cloned.1.call-start
  6.5 0.7 all-gather.3.cloned.1.call-update
  7.9 0.7 compare_bitcast_fusion
  8.6 0.9 multiply_convert_fusion.1
  9.5 96.8 %all-gather.4 = f16[64,128,256]{2,1,0:T(8,128)(2,1)S(1)} all-gather(f16[2,128,256]{2,1,0:T(8,128)(2,1)S(1)} %multiply_convert_fusion.1), channel_id=1, replica_groups=mesh['owner'=32,'slab'=4,'red'=8] {'owner'}, dimensions={0}, use_global_device_ids=true | all-gather | bytes 4325376 | tf_op jit(solution)/shard_map/all_gather | solution.py:111
  106.3 0.0 copy-start.1
  106.3 0.0 copy-start.2
  106.3 1.3 multiply_convert_fusion.pulled
  107.7 0.0 all-gather.3.cloned.1.call-done.integrals
  107.7 0.0 copy-done.1
  107.7 0.0 copy-done.2
  107.7 0.0 copy-start
  107.7 1.6 %copy-done = bf16[64,128,128]{2,1,0:T(8,128)(2,1)S(1)} copy-done((bf16[64,128,128]{2,1,0:T(8,128)(2,1)S(1)}, bf16[64,128,128]{2,1,0:T(8,128)(2,1)}, u32[]{:S(2)}) %copy-start) | copy-done | bytes 2097176
  109.3 2.4 %shard_map.74 = f32[8,128,256]{2,1,0:T(8,128)S(1)} custom-call(s32[1,1,1]{2,1,0:T(1,128)S(6)} %copy.14.live, s32[1,1,12,1,16]{4,3,2,1,0:T(1,128)S(1)} %bitcast.27, s32[1,1,12,1,16]{4,3,2,1,0:T(1,128)S(1)} %bitcast.29, bf16[64,128,128]{2,1,0:T(8,128)(2,1)S(1)} %copy-done, bf16[32,128,256]{2,1,0:T(8,128)(2,1)S(1)} %multiply_convert_fusion.pulled), custom_call_target="tpu_custom_call" | custom-call | flops 805306368 | bytes 1048576 | tf_op jit(solution)/shard_map/pallas_call | solution.py:58
  111.7 1.9 %collective-permute-start = (f32[8,128,256]{2,1,0:T(8,128)S(1)}, f32[8,128,256]{2,1,0:T(8,128)S(1)}, u32[]{:S(2)}, u32[]{:S(2)}) collective-permute-start(f32[8,128,256]{2,1,0:T(8,128)S(1)} %shard_map.74), channel_id=1, source_target_pairs={{0,1},{1,0},{2,3},{3,2},{4,5},{5,4},{6,7},{7,6},{8,9},{9,8},{10,11... | collective-permute-start | bytes 3145736 | tf_op jit(solution)/shard_map/ppermute | solution.py:118
  113.6 2.4 %shard_map.73.mine = f32[8,128,256]{2,1,0:T(8,128)S(1)} custom-call(s32[1,1,1]{2,1,0:T(1,128)S(6)} %copy.14.live, s32[1,1,12,1,16]{4,3,2,1,0:T(1,128)S(1)} %bitcast.28, s32[1,1,12,1,16]{4,3,2,1,0:T(1,128)S(1)} %bitcast.30, bf16[64,128,128]{2,1,0:T(8,128)(2,1)S(1)} %copy-done, bf16[32,128,256]{2,1,0:T(8,128)(2,1)S(1)} %multiply_convert_fusion.pulled), custom_call_target="tpu_custom_call" | custom-call | flops 805306368 | bytes 1048576 | tf_op jit(solution)/shard_map/pallas_call | solution.py:58
  116.0 0.0 copy-start.3
  116.0 0.2 collective-permute-done.came
  116.2 0.1 shard_map.75
  116.3 9.4 %collective-permute-start.1 = (f32[2,2,128,256]{3,2,1,0:T(8,128)S(1)}, f32[2,2,128,256]{3,2,1,0:T(8,128)S(1)}, u32[]{:S(2)}, u32[]{:S(2)}) collective-permute-start(f32[2,2,128,256]{3,2,1,0:T(8,128)S(1)} %get-tuple-element.8), channel_id=1, source_target_pairs={{0,2},{1,7},{2,0},{3,5},{4,6},{5,3},{6,4},{7,1},{8,10},{9,15},{10,... | collective-permute-start | bytes 1572872 | tf_op jit(solution)/shard_map/ppermute | solution.py:122
  125.8 7.1 %collective-permute-done.1 = f32[2,2,128,256]{3,2,1,0:T(8,128)S(1)} collective-permute-done((f32[2,2,128,256]{3,2,1,0:T(8,128)S(1)}, f32[2,2,128,256]{3,2,1,0:T(8,128)S(1)}, u32[]{:S(2)}, u32[]{:S(2)}) %collective-permute-start.1) | collective-permute-done | bytes 524320 | tf_op jit(solution)/shard_map/ppermute | solution.py:122
  133.0 1.9 %collective-permute-start.2 = (f32[2,128,256]{2,1,0:T(8,128)S(1)}, f32[2,128,256]{2,1,0:T(8,128)S(1)}, u32[]{:S(2)}, u32[]{:S(2)}) collective-permute-start(f32[2,128,256]{2,1,0:T(8,128)S(1)} %fusion.1), channel_id=1, source_target_pairs={{0,6},{1,3},{2,4},{3,1},{4,2},{5,7},{6,0},{7,5},{8,14},{9,11},{10,... | collective-permute-start | bytes 786440 | tf_op jit(solution)/shard_map/ppermute | solution.py:123
  134.9 7.5 %collective-permute-done.2 = f32[2,128,256]{2,1,0:T(8,128)S(1)} collective-permute-done((f32[2,128,256]{2,1,0:T(8,128)S(1)}, f32[2,128,256]{2,1,0:T(8,128)S(1)}, u32[]{:S(2)}, u32[]{:S(2)}) %collective-permute-start.2) | collective-permute-done | bytes 262176 | tf_op jit(solution)/shard_map/ppermute | solution.py:123
  142.5 0.0 copy-done.3
  142.5 0.8 fusion.4
  (1 shorter events, 0.0 us)
Async XLA Ops:
  6.5 101.2 %all-gather.3.cloned.1.call-start = ((), (), s32[]{:S(2)}) async-start(), calls=%async_computation | async-start | bytes 2621440 | tf_op jit(solution)/shard_map/all_gather | solution.py:109
  106.3 1.4 copy-start.1
  106.3 1.4 copy-start.2
  107.7 1.6 %copy-start = (bf16[64,128,128]{2,1,0:T(8,128)(2,1)S(1)}, bf16[64,128,128]{2,1,0:T(8,128)(2,1)}, u32[]{:S(2)}) copy-start(bf16[64,128,128]{2,1,0:T(8,128)(2,1)} %all-gather.3.cloned.1.call-done.integrals) | copy-start | bytes 6291460
  111.7 4.6 %collective-permute-start = (f32[8,128,256]{2,1,0:T(8,128)S(1)}, f32[8,128,256]{2,1,0:T(8,128)S(1)}, u32[]{:S(2)}, u32[]{:S(2)}) collective-permute-start(f32[8,128,256]{2,1,0:T(8,128)S(1)} %shard_map.74), channel_id=1, source_target_pairs={{0,1},{1,0},{2,3},{3,2},{4,5},{5,4},{6,7},{7,6},{8,9},{9,8},{10,11... | collective-permute-start | bytes 3145736 | tf_op jit(solution)/shard_map/ppermute | solution.py:118
  116.0 26.5 %copy-start.3 = (f32[2,128,256]{2,1,0:T(8,128)S(1)}, f32[2,128,256]{2,1,0:T(8,128)}, u32[]{:S(2)}) copy-start(f32[2,128,256]{2,1,0:T(8,128)} %param.13) | copy-start | bytes 786436
  116.3 16.6 %collective-permute-start.1 = (f32[2,2,128,256]{3,2,1,0:T(8,128)S(1)}, f32[2,2,128,256]{3,2,1,0:T(8,128)S(1)}, u32[]{:S(2)}, u32[]{:S(2)}) collective-permute-start(f32[2,2,128,256]{3,2,1,0:T(8,128)S(1)} %get-tuple-element.8), channel_id=1, source_target_pairs={{0,2},{1,7},{2,0},{3,5},{4,6},{5,3},{6,4},{7,1},{8,10},{9,15},{10,... | collective-permute-start | bytes 1572872 | tf_op jit(solution)/shard_map/ppermute | solution.py:122
  133.0 9.5 %collective-permute-start.2 = (f32[2,128,256]{2,1,0:T(8,128)S(1)}, f32[2,128,256]{2,1,0:T(8,128)S(1)}, u32[]{:S(2)}, u32[]{:S(2)}) collective-permute-start(f32[2,128,256]{2,1,0:T(8,128)S(1)} %fusion.1), channel_id=1, source_target_pairs={{0,6},{1,3},{2,4},{3,1},{4,2},{5,7},{6,0},{7,5},{8,14},{9,11},{10,... | collective-permute-start | bytes 786440 | tf_op jit(solution)/shard_map/ppermute | solution.py:123
Sparse Core Ops, SparseCore 0:
  10.0 55.1 all-gather.2

commit v3 on v2

--- a/solution.py
+++ b/solution.py
@@ -11,54 +11,61 @@
 SMEM = pltpu.SMEM
 LIFT = 2.0**13
 WIDTH = 4
+UNROLL = 2
 
 
 def place_here():
     return lax.axis_index("red").astype(jnp.int32)
 
 
-def contract(per_chip, flip, live, slots, ints, integrals, pulled, out):
+def contract(per_chip, flip, live, slots, ints, near, far, pulled, out):
     tiles = out.shape[0]
     slot_count = slots.shape[2]
+    owned = near.shape[0] // 2
+    slab, slabs = lax.axis_index("slab").astype(jnp.int32), lax.axis_size("slab")
+    core = lax.rem(place_here(), 2)
     live_count = live[0, 0, 0]
-    half = lax.bitwise_xor(lax.rem(place_here(), 2), flip)
-    groups = lax.div(live_count + (WIDTH - 1), WIDTH)
+    half = lax.bitwise_xor(core, flip)
+    sign = 1 - 2 * core
 
-    def tile(t, _):
-        q = lax.div(t, per_chip) * (2 * per_chip) + half * per_chip + lax.rem(t, per_chip)
+    def integral(index):
+        ahead = lax.bitwise_and(sign * (lax.div(index, owned) - slab), slabs - 1)
+        inside = lax.rem(index, owned)
+        at_near = jnp.where(ahead == slabs - 1, owned, 0) + inside
+        at_far = jnp.where(ahead == 2, owned, 0) + inside
+        is_near = jnp.logical_or(ahead == 0, ahead == slabs - 1)
+        return jnp.where(is_near, near[at_near], far[at_far])
 
-        def some(g):
-            left, right = [], []
-            for w in range(WIDTH):
-                k = jnp.minimum(g * WIDTH + w, slot_count - 1)
-                alive = g * WIDTH + w < live_count
-                block = integrals[ints[0, 0, k, 0, q]]
-                left.append(jnp.where(alive, block, jnp.zeros_like(block)))
-                right.append(pulled[slots[0, 0, k, 0, q]])
-            return jnp.dot(
-                jnp.concatenate(left, axis=1),
-                jnp.concatenate(right, axis=0),
-                preferred_element_type=jnp.float32,
-            )
+    def product(q, groups):
+        left, right = [], []
+        for k in range(groups * WIDTH):
+            block = integral(ints[0, 0, k, 0, q])
+            if k >= (groups - 1) * WIDTH:
+                block = jnp.where(k < live_count, block, jnp.zeros_like(block))
+            left.append(block)
+            right.append(pulled[slots[0, 0, k, 0, q]])
+        return jnp.dot(
+            jnp.concatenate(left, axis=1), jnp.concatenate(right, axis=0), preferred_element_type=jnp.float32
+        )
 
-        out[t] = some(0)
+    for groups in range(1, slot_count // WIDTH + 1):
 
-        def more(g, _):
-            out[t] += some(g)
-            return 0
+        @pl.when(lax.div(live_count + (WIDTH - 1), WIDTH) == groups)
+        def _(groups=groups):
+            def tile(t, _):
+                q = lax.div(t, per_chip) * (2 * per_chip) + half * per_chip + lax.rem(t, per_chip)
+                out[t] = product(q, groups)
+                return 0
 
-        lax.fori_loop(1, groups, more, 0)
-        return 0
-
-    lax.fori_loop(0, tiles, tile, 0)
+            lax.fori_loop(0, tiles, tile, 0, unroll=UNROLL)
 
 
-def call_contract(flip, per_chip, tiles, live, slots, ints, integrals, pulled):
-    rows, columns = integrals.shape[1], pulled.shape[2]
+def call_contract(flip, per_chip, tiles, live, slots, ints, near, far, pulled):
+    rows, columns = near.shape[1], pulled.shape[2]
     return pl.pallas_call(
         functools.partial(contract, per_chip, flip),
         out_shape=jax.ShapeDtypeStruct((tiles, rows, columns), jnp.float32),
-        in_specs=[pl.BlockSpec(memory_space=SMEM)] * 3 + [pl.BlockSpec(memory_space=VMEM)] * 2,
+        in_specs=[pl.BlockSpec(memory_space=SMEM)] * 3 + [pl.BlockSpec(memory_space=VMEM)] * 3,
         out_specs=pl.BlockSpec(memory_space=VMEM),
         compiler_params=pltpu.CompilerParams(vmem_limit_bytes=32 * 2**20),
         cost_estimate=pl.CostEstimate(
@@ -66,7 +73,7 @@
             bytes_accessed=4 * tiles * rows * columns,
             transcendentals=0,
         ),
-    )(live, slots, ints, integrals, pulled)
+    )(live, slots, ints, near, far, pulled)
 
 
 def partner(chip, core, step):
@@ -106,14 +113,25 @@
     wanted = requests.reshape(owners)
     slots, ints = (jnp.transpose(t, (0, 1, 4, 2, 3)) for t in (task_slot, task_integral))
 
-    every_integral = lax.all_gather(integrals, "slab", axis=0, tiled=True)
+    slabs = lax.axis_size("slab")
+    both = ("slab", "red")
+
+    def at(slab, red):
+        return (slab % slabs) * reds + red
+
+    up = [(k, 1 - 2 * (k % 2)) for k in range(reds)]
+    one = [(at(s, k), at(s + d, k)) for s in range(slabs) for k, d in up]
+    two = [(at(s, k), at(s + d, k ^ 1)) for s in range(slabs) for k, d in up]
+    behind = lax.ppermute(integrals, both, one)
+    near = jnp.concatenate([integrals, behind], axis=0)
+    far = lax.ppermute(near, both, two)
     lifted = (amplitudes * jnp.asarray(LIFT, amplitudes.dtype)).astype(jnp.float16)
     every = lax.all_gather(lifted, "owner", axis=0, tiled=True)
     every = every.reshape(owners, -1, *every.shape[1:])
     pulled = jnp.where((wanted == 0)[:, None, None], every[:, 0], every[:, 1])
     pulled = (pulled.astype(jnp.float32) * (1 / LIFT)).astype(jnp.bfloat16)
 
-    tables = (live_tasks, slots, ints, every_integral, pulled)
+    tables = (live_tasks, slots, ints, near, far, pulled)
     other = call_contract(1, per_chip, tiles, *tables)
     came = lax.ppermute(other, "red", [(k, k ^ 1) for k in range(reds)])
     mine = call_contract(0, per_chip, tiles, *tables)

time: 150 us -> 143 us (0.953)
  the two profiles are of different devices: /device:TPU:8 before, /device:TPU:6 now
where the time goes in v3:
time: 143 us
  blocking collectives  98 us (69%)
  waiting for transfers between devices  22.8 us (16%)
  starting transfers between devices  12.7 us (9%)
  Pallas kernels  4.49 us (3%)
  other arithmetic  3.1 us (2%)
    all_gather x1, blocking collectives, on_device(): every = lax.all_gather(lifted, 'owner', axis=0, tiled=True)  98 us
    ppermute x1, waiting for transfers between devices, on_device(): half = lax.ppermute(send, 'red', ways[0])  8.71 us
    ppermute x1, waiting for transfers between devices, on_device(): behind = lax.ppermute(integrals, both, one)  6.97 us
    ppermute x1, waiting for transfers between devices, on_device(): last = lax.ppermute(keep[1] + half[1], 'red', ways[1])  6.73 us
    pallas_call x2, Pallas kernels, call_contract(): pl.pallas_call(functools.partial(contract, per_chip, flip), out_shape=jax...  4.38 us
    ppermute x1, starting transfers between devices, on_device(): behind = lax.ppermute(integrals, both, one)  3.6 us
  transfers between devices with their start and end apart: 5, of which 4 were waited for; matrix products, arithmetic and copies ran while one was open for 2% of the time, Pallas kernels for 2%

profile of v3, /device:TPU:6, one launch (start us, length us, event | category | flops | bytes accessed | tf_op | source)
XLA Modules:
  0.0 143.1 jit_solution(12360013618674181372)
XLA Ops:
  0.0 0.0 copy-start.3
  0.0 3.6 %collective-permute-start = (bf16[16,128,128]{2,1,0:T(8,128)(2,1)}, bf16[16,128,128]{2,1,0:T(8,128)(2,1)S(1)}, u32[]{:S(2)}, u32[]{:S(2)}) collective-permute-start(bf16[16,128,128]{2,1,0:T(8,128)(2,1)} %param.8), channel_id=1, source_target_pairs={{0,8},{1,25},{2,10},{3,27},{4,12},{5,29},{6,14},{7,31},{8,16},{9,1... | collective-permute-start | bytes 1572872 | tf_op jit(solution)/shard_map/ppermute | solution.py:125
  3.6 1.1 constant_dynamic-update-slice_fusion.1
  4.7 0.9 multiply_convert_fusion.1
  5.6 7.0 %collective-permute-done = bf16[16,128,128]{2,1,0:T(8,128)(2,1)S(1)} collective-permute-done((bf16[16,128,128]{2,1,0:T(8,128)(2,1)}, bf16[16,128,128]{2,1,0:T(8,128)(2,1)S(1)}, u32[]{:S(2)}, u32[]{:S(2)}) %collective-permute-start) | collective-permute-done | bytes 524320 | tf_op jit(solution)/shard_map/ppermute | solution.py:125
  12.6 0.1 constant_dynamic-update-slice_fusion.near
  12.7 1.9 %collective-permute-start.1 = (bf16[32,128,128]{2,1,0:T(8,128)(2,1)S(1)}, bf16[32,128,128]{2,1,0:T(8,128)(2,1)S(1)}, u32[]{:S(2)}, u32[]{:S(2)}) collective-permute-start(bf16[32,128,128]{2,1,0:T(8,128)(2,1)S(1)} %constant_dynamic-update-slice_fusion.near), channel_id=1, source_target_pairs={{0,9},{1,24},{2,11},{3,26},{4,13},{5,28},{6,15},{7,30},{8,17},{9,0... | collective-permute-start | bytes 3145736 | tf_op jit(solution)/shard_map/ppermute | solution.py:127
  14.6 98.0 %all-gather.1 = f16[64,128,256]{2,1,0:T(8,128)(2,1)S(1)} all-gather(f16[2,128,256]{2,1,0:T(8,128)(2,1)S(1)} %multiply_convert_fusion.1), channel_id=1, replica_groups=mesh['owner'=32,'slab'=4,'red'=8] {'owner'}, dimensions={0}, use_global_device_ids=true | all-gather | bytes 4325376 | tf_op jit(solution)/shard_map/all_gather | solution.py:129
  112.6 0.0 copy-start
  112.6 0.0 copy-start.1
  113.3 0.0 copy-done.3
  113.3 1.3 multiply_convert_fusion.pulled
  114.6 0.0 collective-permute-done.1.far
  114.6 0.0 copy-done
  114.7 0.0 copy-done.1
  114.7 2.2 %shard_map.74 = f32[8,128,256]{2,1,0:T(8,128)S(1)} custom-call(s32[1,1,1]{2,1,0:T(1,128)S(6)} %copy.15.live, s32[1,1,12,1,16]{4,3,2,1,0:T(1,128)S(1)} %bitcast.27, s32[1,1,12,1,16]{4,3,2,1,0:T(1,128)S(1)} %bitcast.29, bf16[32,128,128]{2,1,0:T(8,128)(2,1)S(1)} %constant_dynamic-update-slice_fusion.near, bf16[32,128,128]{2,1,0:T(8,128)(2,1)S(1)} %collective-permute-done.1.far, ...), custom_call_target="tpu_custom_call" | custom-call | flops 805306368 | bytes 1048576 | tf_op jit(solution)/shard_map/pallas_call | solution.py:65
  116.9 0.0 copy-start.2
  116.9 2.1 %collective-permute-start.2 = (f32[8,128,256]{2,1,0:T(8,128)S(1)}, f32[8,128,256]{2,1,0:T(8,128)S(1)}, u32[]{:S(2)}, u32[]{:S(2)}) collective-permute-start(f32[8,128,256]{2,1,0:T(8,128)S(1)} %shard_map.74), channel_id=1, source_target_pairs={{0,1},{1,0},{2,3},{3,2},{4,5},{5,4},{6,7},{7,6},{8,9},{9,8},{10,11... | collective-permute-start | bytes 3145736 | tf_op jit(solution)/shard_map/ppermute | solution.py:136
  118.9 2.2 %shard_map.73.mine = f32[8,128,256]{2,1,0:T(8,128)S(1)} custom-call(s32[1,1,1]{2,1,0:T(1,128)S(6)} %copy.15.live, s32[1,1,12,1,16]{4,3,2,1,0:T(1,128)S(1)} %bitcast.28, s32[1,1,12,1,16]{4,3,2,1,0:T(1,128)S(1)} %bitcast.30, bf16[32,128,128]{2,1,0:T(8,128)(2,1)S(1)} %constant_dynamic-update-slice_fusion.near, ...), custom_call_target="tpu_custom_call" | custom-call | flops 805306368 | bytes 1048576 | tf_op jit(solution)/shard_map/pallas_call | solution.py:65
  121.1 0.4 collective-permute-done.2.came
  121.6 0.1 shard_map.75
  121.7 2.4 %collective-permute-start.3 = (f32[2,2,128,256]{3,2,1,0:T(8,128)S(1)}, f32[2,2,128,256]{3,2,1,0:T(8,128)S(1)}, u32[]{:S(2)}, u32[]{:S(2)}) collective-permute-start(f32[2,2,128,256]{3,2,1,0:T(8,128)S(1)} %get-tuple-element.8), channel_id=1, source_target_pairs={{0,2},{1,7},{2,0},{3,5},{4,6},{5,3},{6,4},{7,1},{8,10},{9,15},{10,... | collective-permute-start | bytes 1572872 | tf_op jit(solution)/shard_map/ppermute | solution.py:140
  124.0 8.7 %collective-permute-done.3 = f32[2,2,128,256]{3,2,1,0:T(8,128)S(1)} collective-permute-done((f32[2,2,128,256]{3,2,1,0:T(8,128)S(1)}, f32[2,2,128,256]{3,2,1,0:T(8,128)S(1)}, u32[]{:S(2)}, u32[]{:S(2)}) %collective-permute-start.3) | collective-permute-done | bytes 524320 | tf_op jit(solution)/shard_map/ppermute | solution.py:140
  132.8 2.7 %collective-permute-start.4 = (f32[2,128,256]{2,1,0:T(8,128)S(1)}, f32[2,128,256]{2,1,0:T(8,128)S(1)}, u32[]{:S(2)}, u32[]{:S(2)}) collective-permute-start(f32[2,128,256]{2,1,0:T(8,128)S(1)} %fusion.1), channel_id=1, source_target_pairs={{0,6},{1,3},{2,4},{3,1},{4,2},{5,7},{6,0},{7,5},{8,14},{9,11},{10,... | collective-permute-start | bytes 786440 | tf_op jit(solution)/shard_map/ppermute | solution.py:141
  135.5 6.7 %collective-permute-done.4 = f32[2,128,256]{2,1,0:T(8,128)S(1)} collective-permute-done((f32[2,128,256]{2,1,0:T(8,128)S(1)}, f32[2,128,256]{2,1,0:T(8,128)S(1)}, u32[]{:S(2)}, u32[]{:S(2)}) %collective-permute-start.4) | collective-permute-done | bytes 262176 | tf_op jit(solution)/shard_map/ppermute | solution.py:141
  142.3 0.0 copy-done.2
  142.3 0.8 fusion.4
  (2 shorter events, 0.0 us)
Async XLA Ops:
  0.0 113.3 %copy-start.3 = (s32[1,1,1,32]{3,2,1,0:T(1,128)S(1)}, s32[1,1,1,32]{3,2,1,0:T(1,128)}, u32[]{:S(2)}) copy-start(s32[1,1,1,32]{3,2,1,0:T(1,128)} %param.9) | copy-start | bytes 388
  0.0 12.6 %collective-permute-start = (bf16[16,128,128]{2,1,0:T(8,128)(2,1)}, bf16[16,128,128]{2,1,0:T(8,128)(2,1)S(1)}, u32[]{:S(2)}, u32[]{:S(2)}) collective-permute-start(bf16[16,128,128]{2,1,0:T(8,128)(2,1)} %param.8), channel_id=1, source_target_pairs={{0,8},{1,25},{2,10},{3,27},{4,12},{5,29},{6,14},{7,31},{8,16},{9,1... | collective-permute-start | bytes 1572872 | tf_op jit(solution)/shard_map/ppermute | solution.py:125
  12.7 102.0 %collective-permute-start.1 = (bf16[32,128,128]{2,1,0:T(8,128)(2,1)S(1)}, bf16[32,128,128]{2,1,0:T(8,128)(2,1)S(1)}, u32[]{:S(2)}, u32[]{:S(2)}) collective-permute-start(bf16[32,128,128]{2,1,0:T(8,128)(2,1)S(1)} %constant_dynamic-update-slice_fusion.near), channel_id=1, source_target_pairs={{0,9},{1,24},{2,11},{3,26},{4,13},{5,28},{6,15},{7,30},{8,17},{9,0... | collective-permute-start | bytes 3145736 | tf_op jit(solution)/shard_map/ppermute | solution.py:127
  112.6 2.1 %copy-start = (s32[1,1,1,16,12]{3,2,4,1,0:T(1,128)S(1)}, s32[1,1,1,16,12]{3,2,4,1,0:T(1,128)}, u32[]{:S(2)}) copy-start(s32[1,1,1,16,12]{3,2,4,1,0:T(1,128)} %param.10) | copy-start | bytes 2308
  112.6 2.1 %copy-start.1 = (s32[1,1,1,16,12]{3,2,4,1,0:T(1,128)S(1)}, s32[1,1,1,16,12]{3,2,4,1,0:T(1,128)}, u32[]{:S(2)}) copy-start(s32[1,1,1,16,12]{3,2,4,1,0:T(1,128)} %param.11) | copy-start | bytes 2308
  116.9 25.4 %copy-start.2 = (f32[2,128,256]{2,1,0:T(8,128)S(1)}, f32[2,128,256]{2,1,0:T(8,128)}, u32[]{:S(2)}) copy-start(f32[2,128,256]{2,1,0:T(8,128)} %param.13) | copy-start | bytes 786436
  116.9 4.7 %collective-permute-start.2 = (f32[8,128,256]{2,1,0:T(8,128)S(1)}, f32[8,128,256]{2,1,0:T(8,128)S(1)}, u32[]{:S(2)}, u32[]{:S(2)}) collective-permute-start(f32[8,128,256]{2,1,0:T(8,128)S(1)} %shard_map.74), channel_id=1, source_target_pairs={{0,1},{1,0},{2,3},{3,2},{4,5},{5,4},{6,7},{7,6},{8,9},{9,8},{10,11... | collective-permute-start | bytes 3145736 | tf_op jit(solution)/shard_map/ppermute | solution.py:136
  121.7 11.1 %collective-permute-start.3 = (f32[2,2,128,256]{3,2,1,0:T(8,128)S(1)}, f32[2,2,128,256]{3,2,1,0:T(8,128)S(1)}, u32[]{:S(2)}, u32[]{:S(2)}) collective-permute-start(f32[2,2,128,256]{3,2,1,0:T(8,128)S(1)} %get-tuple-element.8), channel_id=1, source_target_pairs={{0,2},{1,7},{2,0},{3,5},{4,6},{5,3},{6,4},{7,1},{8,10},{9,15},{10,... | collective-permute-start | bytes 1572872 | tf_op jit(solution)/shard_map/ppermute | solution.py:140
  132.8 9.5 %collective-permute-start.4 = (f32[2,128,256]{2,1,0:T(8,128)S(1)}, f32[2,128,256]{2,1,0:T(8,128)S(1)}, u32[]{:S(2)}, u32[]{:S(2)}) collective-permute-start(f32[2,128,256]{2,1,0:T(8,128)S(1)} %fusion.1), channel_id=1, source_target_pairs={{0,6},{1,3},{2,4},{3,1},{4,2},{5,7},{6,0},{7,5},{8,14},{9,11},{10,... | collective-permute-start | bytes 786440 | tf_op jit(solution)/shard_map/ppermute | solution.py:141

commit v4 on v3

--- a/solution.py
+++ b/solution.py
@@ -18,28 +18,28 @@
     return lax.axis_index("red").astype(jnp.int32)
 
 
-def contract(per_chip, flip, live, slots, ints, near, far, pulled, out):
+def contract(per_chip, flip, live, slots, ints, near, far, next_given, far_given, pulled, out):
     tiles = out.shape[0]
     slot_count = slots.shape[2]
-    owned = near.shape[0] // 2
+    owned = next_given.shape[0]
     slab, slabs = lax.axis_index("slab").astype(jnp.int32), lax.axis_size("slab")
     core = lax.rem(place_here(), 2)
     live_count = live[0, 0, 0]
     half = lax.bitwise_xor(core, flip)
-    sign = 1 - 2 * core
 
-    def integral(index):
-        ahead = lax.bitwise_and(sign * (lax.div(index, owned) - slab), slabs - 1)
+    def integral(index, fetcher):
+        ahead = lax.bitwise_and(lax.div(index, owned) - slab, slabs - 1)
         inside = lax.rem(index, owned)
-        at_near = jnp.where(ahead == slabs - 1, owned, 0) + inside
-        at_far = jnp.where(ahead == 2, owned, 0) + inside
-        is_near = jnp.logical_or(ahead == 0, ahead == slabs - 1)
-        return jnp.where(is_near, near[at_near], far[at_far])
+        at_far = jnp.where(ahead == 3, owned, 0) + inside
+        if fetcher:
+            at_near = jnp.where(ahead == 1, owned, 0) + inside
+            return jnp.where(ahead < 2, near[at_near], far[at_far])
+        return jnp.where(ahead == 0, near[inside], jnp.where(ahead == 1, next_given[inside], far_given[at_far]))
 
-    def product(q, groups):
+    def product(q, groups, fetcher):
         left, right = [], []
         for k in range(groups * WIDTH):
-            block = integral(ints[0, 0, k, 0, q])
+            block = integral(ints[0, 0, k, 0, q], fetcher)
             if k >= (groups - 1) * WIDTH:
                 block = jnp.where(k < live_count, block, jnp.zeros_like(block))
             left.append(block)
@@ -48,24 +48,26 @@
             jnp.concatenate(left, axis=1), jnp.concatenate(right, axis=0), preferred_element_type=jnp.float32
         )
 
+    live_groups = lax.div(live_count + (WIDTH - 1), WIDTH)
     for groups in range(1, slot_count // WIDTH + 1):
+        for fetcher in (0, 1):
 
-        @pl.when(lax.div(live_count + (WIDTH - 1), WIDTH) == groups)
-        def _(groups=groups):
-            def tile(t, _):
-                q = lax.div(t, per_chip) * (2 * per_chip) + half * per_chip + lax.rem(t, per_chip)
-                out[t] = product(q, groups)
-                return 0
+            @pl.when(jnp.logical_and(live_groups == groups, core == fetcher))
+            def _(groups=groups, fetcher=fetcher):
+                def tile(t, _):
+                    q = lax.div(t, per_chip) * (2 * per_chip) + half * per_chip + lax.rem(t, per_chip)
+                    out[t] = product(q, groups, fetcher)
+                    return 0
 
-            lax.fori_loop(0, tiles, tile, 0, unroll=UNROLL)
+                lax.fori_loop(0, tiles, tile, 0, unroll=UNROLL)
 
 
-def call_contract(flip, per_chip, tiles, live, slots, ints, near, far, pulled):
-    rows, columns = near.shape[1], pulled.shape[2]
+def call_contract(flip, per_chip, tiles, live, slots, ints, *blocks):
+    rows, columns = blocks[0].shape[1], blocks[-1].shape[2]
     return pl.pallas_call(
         functools.partial(contract, per_chip, flip),
         out_shape=jax.ShapeDtypeStruct((tiles, rows, columns), jnp.float32),
-        in_specs=[pl.BlockSpec(memory_space=SMEM)] * 3 + [pl.BlockSpec(memory_space=VMEM)] * 3,
+        in_specs=[pl.BlockSpec(memory_space=SMEM)] * 3 + [pl.BlockSpec(memory_space=VMEM)] * len(blocks),
         out_specs=pl.BlockSpec(memory_space=VMEM),
         compiler_params=pltpu.CompilerParams(vmem_limit_bytes=32 * 2**20),
         cost_estimate=pl.CostEstimate(
@@ -73,7 +75,7 @@
             bytes_accessed=4 * tiles * rows * columns,
             transcendentals=0,
         ),
-    )(live, slots, ints, near, far, pulled)
+    )(live, slots, ints, *blocks)
 
 
 def partner(chip, core, step):
@@ -119,19 +121,23 @@
     def at(slab, red):
         return (slab % slabs) * reds + red
 
-    up = [(k, 1 - 2 * (k % 2)) for k in range(reds)]
-    one = [(at(s, k), at(s + d, k)) for s in range(slabs) for k, d in up]
-    two = [(at(s, k), at(s + d, k ^ 1)) for s in range(slabs) for k, d in up]
-    behind = lax.ppermute(integrals, both, one)
-    near = jnp.concatenate([integrals, behind], axis=0)
+    fetchers = range(1, reds, 2)
+    one = [(at(s + 1, k), at(s, k)) for s in range(slabs) for k in fetchers]
+    two = [(at(s + 2, k), at(s, k)) for s in range(slabs) for k in fetchers]
+    give = [(k, k ^ 1) for k in fetchers]
+    beyond = lax.ppermute(integrals, both, one)
+    near = jnp.concatenate([integrals, beyond], axis=0)
     far = lax.ppermute(near, both, two)
+    next_given = lax.ppermute(beyond, "red", give)
     lifted = (amplitudes * jnp.asarray(LIFT, amplitudes.dtype)).astype(jnp.float16)
     every = lax.all_gather(lifted, "owner", axis=0, tiled=True)
+    every, far = lax.optimization_barrier((every, far))
+    far_given = lax.ppermute(far, "red", give)
     every = every.reshape(owners, -1, *every.shape[1:])
     pulled = jnp.where((wanted == 0)[:, None, None], every[:, 0], every[:, 1])
     pulled = (pulled.astype(jnp.float32) * (1 / LIFT)).astype(jnp.bfloat16)
 
-    tables = (live_tasks, slots, ints, near, far, pulled)
+    tables = (live_tasks, slots, ints, near, far, next_given, far_given, pulled)
     other = call_contract(1, per_chip, tiles, *tables)
     came = lax.ppermute(other, "red", [(k, k ^ 1) for k in range(reds)])
     mine = call_contract(0, per_chip, tiles, *tables)

time: 143 us -> 137 us (0.958)
  waiting for transfers between devices: 22.8 us -> 17.3 us
  starting transfers between devices: 12.7 us -> 11.1 us
    ppermute x1 -> x3, waiting for transfers between devices: 6.97 us -> 1.21 us  [the longest x1 1.21 us: on_device(): next_given = lax.ppermute(beyond, 'red', give)]
    ppermute x1 -> x3, starting transfers between devices: 3.6 us -> 3.52 us  [the longest x1 1.42 us: on_device(): far_given = lax.ppermute(far, 'red', give)]
  transfers between devices with their start and end apart: 5 -> 7, of which waited for: 4 -> 4; matrix products, arithmetic and copies ran while one was open for 2% -> 2% of each run, Pallas kernels for 2% -> 2%
where the time goes in v4:
time: 137 us; the launch traced here: 136 us
  blocking collectives  97.8 us (71%)
  waiting for transfers between devices  17.3 us (13%)
  starting transfers between devices  11.1 us (8%)
  Pallas kernels  4.77 us (3%)
  other arithmetic  3.1 us (2%)
    all_gather x1, blocking collectives, on_device(): every = lax.all_gather(lifted, 'owner', axis=0, tiled=True)  97.8 us
    ppermute x1, waiting for transfers between devices, on_device(): half = lax.ppermute(send, 'red', ways[0])  8.33 us
    ppermute x1, waiting for transfers between devices, on_device(): last = lax.ppermute(keep[1] + half[1], 'red', ways[1])  7.45 us
    pallas_call x2, Pallas kernels, call_contract(): pl.pallas_call(functools.partial(contract, per_chip, flip), out_shape=jax...  4.67 us
  transfers between devices with their start and end apart: 7, of which 4 were waited for; matrix products, arithmetic and copies ran while one was open for 2% of the time, Pallas kernels for 2%

profile of v4, /device:TPU:6, one launch (start us, length us, event | category | flops | bytes accessed | tf_op | source)
XLA Modules:
  0.0 136.0 jit_solution(7870902409152494005)
XLA Ops:
  0.0 0.0 copy-start.3
  0.0 0.8 collective-permute-start
  0.8 1.1 constant_dynamic-update-slice_fusion.1
  1.9 0.9 multiply_convert_fusion.1
  2.8 0.0 collective-permute-done
  2.9 0.1 constant_dynamic-update-slice_fusion.near
  2.9 0.7 collective-permute-start.1
  3.7 97.8 %all-gather.1 = f16[64,128,256]{2,1,0:T(8,128)(2,1)S(1)} all-gather(f16[2,128,256]{2,1,0:T(8,128)(2,1)S(1)} %multiply_convert_fusion.1), channel_id=1, replica_groups=mesh['owner'=32,'slab'=4,'red'=8] {'owner'}, dimensions={0}, use_global_device_ids=true | all-gather | bytes 4325376 | tf_op jit(solution)/shard_map/all_gather | solution.py:133
  101.5 0.0 copy-start
  101.5 0.0 copy-start.1
  101.5 0.0 collective-permute-done.1.far
  101.5 1.4 %collective-permute-start.3 = (bf16[32,128,128]{2,1,0:T(8,128)(2,1)S(1)}, bf16[32,128,128]{2,1,0:T(8,128)(2,1)S(1)}, u32[]{:S(2)}, u32[]{:S(2)}) collective-permute-start(bf16[32,128,128]{2,1,0:T(8,128)(2,1)S(1)} %collective-permute-done.1.far), channel_id=1, source_target_pairs={{1,0},{3,2},{5,4},{7,6},{9,8},{11,10},{13,12},{15,14},{17,16},{19,... | collective-permute-start | bytes 3145736 | tf_op jit(solution)/shard_map/ppermute | solution.py:135
  103.6 1.3 collective-permute-start.2
  104.9 0.0 copy-done.3
  104.9 1.3 multiply_convert_fusion.pulled
  106.2 1.2 collective-permute-done.2.next_given
  107.4 0.0 collective-permute-done.3.far_given
  107.4 0.0 copy-done
  107.4 0.0 copy-done.1
  107.4 2.3 %shard_map.74 = f32[8,128,256]{2,1,0:T(8,128)S(1)} custom-call(s32[1,1,1]{2,1,0:T(1,128)S(6)} %copy.15.live, s32[1,1,12,1,16]{4,3,2,1,0:T(1,128)S(1)} %bitcast.27, s32[1,1,12,1,16]{4,3,2,1,0:T(1,128)S(1)} %bitcast.29, bf16[32,128,128]{2,1,0:T(8,128)(2,1)S(1)} %constant_dynamic-update-slice_fusion.near, bf16[32,128,128]{2,1,0:T(8,128)(2,1)S(1)} %collective-permute-done.1.far, ...), custom_call_target="tpu_custom_call" | custom-call | flops 805306368 | bytes 1048576 | tf_op jit(solution)/shard_map/pallas_call | solution.py:67
  109.8 0.0 copy-start.2
  109.8 2.1 %collective-permute-start.4 = (f32[8,128,256]{2,1,0:T(8,128)S(1)}, f32[8,128,256]{2,1,0:T(8,128)S(1)}, u32[]{:S(2)}, u32[]{:S(2)}) collective-permute-start(f32[8,128,256]{2,1,0:T(8,128)S(1)} %shard_map.74), channel_id=1, source_target_pairs={{0,1},{1,0},{2,3},{3,2},{4,5},{5,4},{6,7},{7,6},{8,9},{9,8},{10,11... | collective-permute-start | bytes 3145736 | tf_op jit(solution)/shard_map/ppermute | solution.py:142
  111.9 2.3 %shard_map.73.mine = f32[8,128,256]{2,1,0:T(8,128)S(1)} custom-call(s32[1,1,1]{2,1,0:T(1,128)S(6)} %copy.15.live, s32[1,1,12,1,16]{4,3,2,1,0:T(1,128)S(1)} %bitcast.28, s32[1,1,12,1,16]{4,3,2,1,0:T(1,128)S(1)} %bitcast.30, bf16[32,128,128]{2,1,0:T(8,128)(2,1)S(1)} %constant_dynamic-update-slice_fusion.near, ...), custom_call_target="tpu_custom_call" | custom-call | flops 805306368 | bytes 1048576 | tf_op jit(solution)/shard_map/pallas_call | solution.py:67
  114.2 0.3 collective-permute-done.4.came
  114.5 0.1 shard_map.75
  114.6 2.7 %collective-permute-start.5 = (f32[2,2,128,256]{3,2,1,0:T(8,128)S(1)}, f32[2,2,128,256]{3,2,1,0:T(8,128)S(1)}, u32[]{:S(2)}, u32[]{:S(2)}) collective-permute-start(f32[2,2,128,256]{3,2,1,0:T(8,128)S(1)} %get-tuple-element.12), channel_id=1, source_target_pairs={{0,2},{1,7},{2,0},{3,5},{4,6},{5,3},{6,4},{7,1},{8,10},{9,15},{10,... | collective-permute-start | bytes 1572872 | tf_op jit(solution)/shard_map/ppermute | solution.py:146
  117.3 8.3 %collective-permute-done.5 = f32[2,2,128,256]{3,2,1,0:T(8,128)S(1)} collective-permute-done((f32[2,2,128,256]{3,2,1,0:T(8,128)S(1)}, f32[2,2,128,256]{3,2,1,0:T(8,128)S(1)}, u32[]{:S(2)}, u32[]{:S(2)}) %collective-permute-start.5) | collective-permute-done | bytes 524320 | tf_op jit(solution)/shard_map/ppermute | solution.py:146
  125.7 2.0 %collective-permute-start.6 = (f32[2,128,256]{2,1,0:T(8,128)S(1)}, f32[2,128,256]{2,1,0:T(8,128)S(1)}, u32[]{:S(2)}, u32[]{:S(2)}) collective-permute-start(f32[2,128,256]{2,1,0:T(8,128)S(1)} %fusion.1), channel_id=1, source_target_pairs={{0,6},{1,3},{2,4},{3,1},{4,2},{5,7},{6,0},{7,5},{8,14},{9,11},{10,... | collective-permute-start | bytes 786440 | tf_op jit(solution)/shard_map/ppermute | solution.py:147
  127.7 7.5 %collective-permute-done.6 = f32[2,128,256]{2,1,0:T(8,128)S(1)} collective-permute-done((f32[2,128,256]{2,1,0:T(8,128)S(1)}, f32[2,128,256]{2,1,0:T(8,128)S(1)}, u32[]{:S(2)}, u32[]{:S(2)}) %collective-permute-start.6) | collective-permute-done | bytes 262176 | tf_op jit(solution)/shard_map/ppermute | solution.py:147
  135.2 0.0 copy-done.2
  135.2 0.8 fusion.4
  (2 shorter events, 0.0 us)
Async XLA Ops:
  0.0 104.9 %copy-start.3 = (s32[1,1,1,32]{3,2,1,0:T(1,128)S(1)}, s32[1,1,1,32]{3,2,1,0:T(1,128)}, u32[]{:S(2)}) copy-start(s32[1,1,1,32]{3,2,1,0:T(1,128)} %param.9) | copy-start | bytes 388
  0.0 2.8 %collective-permute-start = (bf16[16,128,128]{2,1,0:T(8,128)(2,1)}, bf16[16,128,128]{2,1,0:T(8,128)(2,1)S(1)}, u32[]{:S(2)}, u32[]{:S(2)}) collective-permute-start(bf16[16,128,128]{2,1,0:T(8,128)(2,1)} %param.8), channel_id=1, source_target_pairs={{9,1},{11,3},{13,5},{15,7},{17,9},{19,11},{21,13},{23,15},{25,17},... | collective-permute-start | bytes 1572872 | tf_op jit(solution)/shard_map/ppermute | solution.py:128
  2.9 98.6 %collective-permute-start.1 = (bf16[32,128,128]{2,1,0:T(8,128)(2,1)S(1)}, bf16[32,128,128]{2,1,0:T(8,128)(2,1)S(1)}, u32[]{:S(2)}, u32[]{:S(2)}) collective-permute-start(bf16[32,128,128]{2,1,0:T(8,128)(2,1)S(1)} %constant_dynamic-update-slice_fusion.near), channel_id=1, source_target_pairs={{17,1},{19,3},{21,5},{23,7},{25,9},{27,11},{29,13},{31,15},{1,17},... | collective-permute-start | bytes 3145736 | tf_op jit(solution)/shard_map/ppermute | solution.py:130
  101.5 6.0 %copy-start = (s32[1,1,1,16,12]{3,2,4,1,0:T(1,128)S(1)}, s32[1,1,1,16,12]{3,2,4,1,0:T(1,128)}, u32[]{:S(2)}) copy-start(s32[1,1,1,16,12]{3,2,4,1,0:T(1,128)} %param.10) | copy-start | bytes 2308
  101.5 6.0 %copy-start.1 = (s32[1,1,1,16,12]{3,2,4,1,0:T(1,128)S(1)}, s32[1,1,1,16,12]{3,2,4,1,0:T(1,128)}, u32[]{:S(2)}) copy-start(s32[1,1,1,16,12]{3,2,4,1,0:T(1,128)} %param.11) | copy-start | bytes 2308
  101.5 5.9 %collective-permute-start.3 = (bf16[32,128,128]{2,1,0:T(8,128)(2,1)S(1)}, bf16[32,128,128]{2,1,0:T(8,128)(2,1)S(1)}, u32[]{:S(2)}, u32[]{:S(2)}) collective-permute-start(bf16[32,128,128]{2,1,0:T(8,128)(2,1)S(1)} %collective-permute-done.1.far), channel_id=1, source_target_pairs={{1,0},{3,2},{5,4},{7,6},{9,8},{11,10},{13,12},{15,14},{17,16},{19,... | collective-permute-start | bytes 3145736 | tf_op jit(solution)/shard_map/ppermute | solution.py:135
  103.6 3.9 %collective-permute-start.2 = (bf16[16,128,128]{2,1,0:T(8,128)(2,1)S(1)}, bf16[16,128,128]{2,1,0:T(8,128)(2,1)S(1)}, u32[]{:S(2)}, u32[]{:S(2)}) collective-permute-start(bf16[16,128,128]{2,1,0:T(8,128)(2,1)S(1)} %collective-permute-done), channel_id=1, source_target_pairs={{1,0},{3,2},{5,4},{7,6},{9,8},{11,10},{13,12},{15,14},{17,16},{19,... | collective-permute-start | bytes 1572872 | tf_op jit(solution)/shard_map/ppermute | solution.py:131
  109.8 25.4 %copy-start.2 = (f32[2,128,256]{2,1,0:T(8,128)S(1)}, f32[2,128,256]{2,1,0:T(8,128)}, u32[]{:S(2)}) copy-start(f32[2,128,256]{2,1,0:T(8,128)} %param.13) | copy-start | bytes 786436
  109.8 4.7 %collective-permute-start.4 = (f32[8,128,256]{2,1,0:T(8,128)S(1)}, f32[8,128,256]{2,1,0:T(8,128)S(1)}, u32[]{:S(2)}, u32[]{:S(2)}) collective-permute-start(f32[8,128,256]{2,1,0:T(8,128)S(1)} %shard_map.74), channel_id=1, source_target_pairs={{0,1},{1,0},{2,3},{3,2},{4,5},{5,4},{6,7},{7,6},{8,9},{9,8},{10,11... | collective-permute-start | bytes 3145736 | tf_op jit(solution)/shard_map/ppermute | solution.py:142
  114.6 11.1 %collective-permute-start.5 = (f32[2,2,128,256]{3,2,1,0:T(8,128)S(1)}, f32[2,2,128,256]{3,2,1,0:T(8,128)S(1)}, u32[]{:S(2)}, u32[]{:S(2)}) collective-permute-start(f32[2,2,128,256]{3,2,1,0:T(8,128)S(1)} %get-tuple-element.12), channel_id=1, source_target_pairs={{0,2},{1,7},{2,0},{3,5},{4,6},{5,3},{6,4},{7,1},{8,10},{9,15},{10,... | collective-permute-start | bytes 1572872 | tf_op jit(solution)/shard_map/ppermute | solution.py:146
  125.7 9.5 %collective-permute-start.6 = (f32[2,128,256]{2,1,0:T(8,128)S(1)}, f32[2,128,256]{2,1,0:T(8,128)S(1)}, u32[]{:S(2)}, u32[]{:S(2)}) collective-permute-start(f32[2,128,256]{2,1,0:T(8,128)S(1)} %fusion.1), channel_id=1, source_target_pairs={{0,6},{1,3},{2,4},{3,1},{4,2},{5,7},{6,0},{7,5},{8,14},{9,11},{10,... | collective-permute-start | bytes 786440 | tf_op jit(solution)/shard_map/ppermute | solution.py:147

commit v5 on v4

--- a/solution.py
+++ b/solution.py
@@ -12,6 +12,8 @@
 LIFT = 2.0**13
 WIDTH = 4
 UNROLL = 2
+TOP = 32760.0
+EXTRA = 16
 
 
 def place_here():
@@ -82,6 +84,21 @@
     return chip ^ 1 if (core + step) % 2 == 0 else 3 - chip
 
 
+def encode(values, target):
+    rows, columns = values.shape
+    peak = jnp.maximum(jnp.max(jnp.abs(values), axis=0, keepdims=True), 1e-30)
+    exponent = jnp.floor(jnp.log2(peak)) + 1.0
+    scaled = values * (jnp.exp2(-exponent) * TOP)
+    target[:rows] = jnp.floor(scaled + 0.5).astype(jnp.int32).astype(jnp.int16)
+    target[rows:] = jnp.broadcast_to(exponent, (EXTRA, columns)).astype(jnp.int32).astype(jnp.int16)
+
+
+def decode(source):
+    rows = source.shape[0] - EXTRA
+    exponent = source[rows:].astype(jnp.int32).astype(jnp.float32)[:1]
+    return source[:rows].astype(jnp.int32).astype(jnp.float32) * (jnp.exp2(exponent) * (1 / TOP))
+
+
 def combine(per_chip, mine, came, keep, send):
     place = place_here()
     here, core = lax.div(place, 2), lax.rem(place, 2)
@@ -89,21 +106,34 @@
     first = jnp.where(core == 0, near, 3 - here)
     second = jnp.where(core == 0, 3 - here, near)
     across = lax.bitwise_xor(here, 2)
-    for block, target, at in ((first, send, 0), (across, send, 1), (here, keep, 0), (second, keep, 1)):
+    for at, block in enumerate((first, across)):
         for j in range(per_chip):
             t = block * per_chip + j
-            target[at, j] = mine[t] + came[t]
-
-
-def call_combine(per_chip, mine, came):
-    shape = jax.ShapeDtypeStruct((2, per_chip, *mine.shape[1:]), jnp.float32)
+            encode(mine[t] + came[t], send.at[at, j])
+    for at, block in enumerate((here, second)):
+        for j in range(per_chip):
+            t = block * per_chip + j
+            keep[at, j] = mine[t] + came[t]
+
+
+def pass_on(keep, half, send):
+    for j in range(keep.shape[1]):
+        encode(keep[1, j] + decode(half.at[1, j]), send.at[j])
+
+
+def finish(keep, half, last, denominators, out):
+    for j in range(keep.shape[1]):
+        out[j] = (keep[0, j] + decode(half.at[0, j]) + decode(last.at[j])) / denominators[j]
+
+
+def on_chip(kernel, shapes, *arrays):
     return pl.pallas_call(
-        functools.partial(combine, per_chip),
-        out_shape=(shape, shape),
-        in_specs=[pl.BlockSpec(memory_space=VMEM)] * 2,
-        out_specs=(pl.BlockSpec(memory_space=VMEM),) * 2,
+        kernel,
+        out_shape=shapes,
+        in_specs=[pl.BlockSpec(memory_space=VMEM)] * len(arrays),
+        out_specs=jax.tree.map(lambda _: pl.BlockSpec(memory_space=VMEM), shapes),
         compiler_params=pltpu.CompilerParams(vmem_limit_bytes=32 * 2**20),
-    )(mine, came)
+    )(*arrays)
 
 
 def on_device(amplitudes, integrals, requests, task_slot, task_integral, live_tasks, denominators):
@@ -141,11 +171,17 @@
     other = call_contract(1, per_chip, tiles, *tables)
     came = lax.ppermute(other, "red", [(k, k ^ 1) for k in range(reds)])
     mine = call_contract(0, per_chip, tiles, *tables)
-    keep, send = call_combine(per_chip, mine, came)
+    rows, columns = mine.shape[1:]
+    whole = jax.ShapeDtypeStruct((2, per_chip, rows, columns), jnp.float32)
+    coded = jax.ShapeDtypeStruct((2, per_chip, rows + EXTRA, columns), jnp.int16)
+    one_coded = jax.ShapeDtypeStruct(coded.shape[1:], jnp.int16)
+    keep, send = on_chip(functools.partial(combine, per_chip), (whole, coded), mine, came)
     ways = [[(k, 2 * partner(k // 2, k % 2, step) + k % 2) for k in range(reds)] for step in range(2)]
     half = lax.ppermute(send, "red", ways[0])
-    last = lax.ppermute(keep[1] + half[1], "red", ways[1])
-    return (keep[0] + half[0] + last) / denominators
+    last = lax.ppermute(on_chip(pass_on, one_coded, keep, half), "red", ways[1])
+    return on_chip(
+        finish, jax.ShapeDtypeStruct(denominators.shape, jnp.float32), keep, half, last, denominators
+    )
 
 
 def solution(mesh):

time: 137 us -> 134 us (0.978)
  waiting for transfers between devices: 17.3 us -> 13.1 us
    ppermute x1, waiting for transfers between devices: 8.33 us -> 5.39 us  [on_device(): half = lax.ppermute(send, 'red', ways[0])]
    ppermute x1, waiting for transfers between devices: 7.45 us -> 5.85 us  [on_device(): last = lax.ppermute(on_chip(pass_on, one_coded, keep, half), 'red', ways[1])]
  transfers between devices with their start and end apart: 7 -> 7, of which waited for: 4 -> 4; matrix products, arithmetic and copies ran while one was open for 2% -> 3% of each run, Pallas kernels for 2% -> 1%
where the time goes in v5:
time: 134 us; the launch traced here: 132 us
  blocking collectives  97.8 us (73%)
  waiting for transfers between devices  13.1 us (10%)
  starting transfers between devices  12 us (9%)
  Pallas kernels  4.84 us (4%)
  other arithmetic  2.27 us (2%)
    all_gather x1, blocking collectives, on_device(): every = lax.all_gather(lifted, 'owner', axis=0, tiled=True)  97.8 us
    ppermute x1, waiting for transfers between devices, on_device(): last = lax.ppermute(on_chip(pass_on, one_coded, keep, half), 'red', ways[1])  5.85 us
    ppermute x1, waiting for transfers between devices, on_device(): half = lax.ppermute(send, 'red', ways[0])  5.39 us
    pallas_call x2, Pallas kernels, call_contract(): pl.pallas_call(functools.partial(contract, per_chip, flip), out_shape=jax...  3.7 us
    ppermute x1, starting transfers between devices, on_device(): half = lax.ppermute(send, 'red', ways[0])  3.22 us
  transfers between devices with their start and end apart: 7, of which 4 were waited for; matrix products, arithmetic and copies ran while one was open for 3% of the time, Pallas kernels for 1%

profile of v5, /device:TPU:6, one launch (start us, length us, event | category | flops | bytes accessed | tf_op | source)
XLA Modules:
  0.0 132.0 jit_solution(15200843399383973712)
XLA Ops:
  0.0 0.0 copy-start.3
  0.0 0.8 collective-permute-start
  0.8 1.1 constant_dynamic-update-slice_fusion.1
  1.9 0.9 multiply_convert_fusion.1
  2.8 0.0 collective-permute-done
  2.9 0.1 constant_dynamic-update-slice_fusion.near
  2.9 0.7 collective-permute-start.1
  3.7 97.8 %all-gather.1 = f16[64,128,256]{2,1,0:T(8,128)(2,1)S(1)} all-gather(f16[2,128,256]{2,1,0:T(8,128)(2,1)S(1)} %multiply_convert_fusion.1), channel_id=1, replica_groups=mesh['owner'=32,'slab'=4,'red'=8] {'owner'}, dimensions={0}, use_global_device_ids=true | all-gather | bytes 4325376 | tf_op jit(solution)/shard_map/all_gather | solution.py:163
  101.5 0.0 copy-start.1
  101.5 0.0 copy-start.2
  101.5 0.0 collective-permute-done.1.far
  101.5 1.4 %collective-permute-start.3 = (bf16[32,128,128]{2,1,0:T(8,128)(2,1)S(1)}, bf16[32,128,128]{2,1,0:T(8,128)(2,1)S(1)}, u32[]{:S(2)}, u32[]{:S(2)}) collective-permute-start(bf16[32,128,128]{2,1,0:T(8,128)(2,1)S(1)} %collective-permute-done.1.far), channel_id=1, source_target_pairs={{1,0},{3,2},{5,4},{7,6},{9,8},{11,10},{13,12},{15,14},{17,16},{19,... | collective-permute-start | bytes 3145736 | tf_op jit(solution)/shard_map/ppermute | solution.py:165
  103.6 1.3 collective-permute-start.2
  104.9 0.0 copy-done.3
  104.9 1.3 %multiply_convert_fusion.pulled = bf16[32,128,256]{2,1,0:T(8,128)(2,1)S(1)} fusion(f16[32,2,128,256]{3,2,1,0:T(8,128)(2,1)S(1)} %bitcast.23, pred[32]{0:T(512)(128)(4,1)S(1)} %compare_bitcast_fusion), kind=kLoop, calls=%fused_computation | loop fusion | flops 4194304 | bytes 6291488 | tf_op jit(solution)/shard_map/convert_element_type | solution.py:168
  106.2 1.2 collective-permute-done.2.next_given
  107.4 0.0 collective-permute-done.3.far_given
  107.4 0.0 copy-done.1
  107.4 0.0 copy-done.2
  107.4 1.9 %shard_map.74 = f32[8,128,256]{2,1,0:T(8,128)S(1)} custom-call(s32[1,1,1]{2,1,0:T(1,128)S(6)} %copy.15.live, s32[1,1,12,1,16]{4,3,2,1,0:T(1,128)S(1)} %bitcast.19, s32[1,1,12,1,16]{4,3,2,1,0:T(1,128)S(1)} %bitcast.21, bf16[32,128,128]{2,1,0:T(8,128)(2,1)S(1)} %constant_dynamic-update-slice_fusion.near, bf16[32,128,128]{2,1,0:T(8,128)(2,1)S(1)} %collective-permute-done.1.far, ...), custom_call_target="tpu_custom_call" | custom-call | flops 805306368 | bytes 1048576 | tf_op jit(solution)/shard_map/pallas_call | solution.py:69
  109.3 0.0 copy-start
  109.3 2.2 %collective-permute-start.4 = (f32[8,128,256]{2,1,0:T(8,128)S(1)}, f32[8,128,256]{2,1,0:T(8,128)S(1)}, u32[]{:S(2)}, u32[]{:S(2)}) collective-permute-start(f32[8,128,256]{2,1,0:T(8,128)S(1)} %shard_map.74), channel_id=1, source_target_pairs={{0,1},{1,0},{2,3},{3,2},{4,5},{5,4},{6,7},{7,6},{8,9},{9,8},{10,11... | collective-permute-start | bytes 3145736 | tf_op jit(solution)/shard_map/ppermute | solution.py:172
  111.5 1.9 %shard_map.73.mine = f32[8,128,256]{2,1,0:T(8,128)S(1)} custom-call(s32[1,1,1]{2,1,0:T(1,128)S(6)} %copy.15.live, s32[1,1,12,1,16]{4,3,2,1,0:T(1,128)S(1)} %bitcast.20, s32[1,1,12,1,16]{4,3,2,1,0:T(1,128)S(1)} %bitcast.22, bf16[32,128,128]{2,1,0:T(8,128)(2,1)S(1)} %constant_dynamic-update-slice_fusion.near, ...), custom_call_target="tpu_custom_call" | custom-call | flops 805306368 | bytes 1048576 | tf_op jit(solution)/shard_map/pallas_call | solution.py:69
  113.3 0.7 collective-permute-done.4.came
  114.0 0.2 shard_map.75
  114.2 3.2 %collective-permute-start.5 = (s16[2,2,144,256]{3,2,1,0:T(8,128)(2,1)S(1)}, s16[2,2,144,256]{3,2,1,0:T(8,128)(2,1)S(1)}, u32[]{:S(2)}, u32[]{:S(2)}) collective-permute-start(s16[2,2,144,256]{3,2,1,0:T(8,128)(2,1)S(1)} %get-tuple-element.12), channel_id=1, source_target_pairs={{0,2},{1,7},{2,0},{3,5},{4,6},{5,3},{6,4},{7,1},{8,10},{9,15},{10,... | collective-permute-start | bytes 884744 | tf_op jit(solution)/shard_map/ppermute | solution.py:180
  117.5 5.4 %collective-permute-done.5.half = s16[2,2,144,256]{3,2,1,0:T(8,128)(2,1)S(1)} collective-permute-done((s16[2,2,144,256]{3,2,1,0:T(8,128)(2,1)S(1)}, s16[2,2,144,256]{3,2,1,0:T(8,128)(2,1)S(1)}, u32[]{:S(2)}, u32[]{:S(2)}) %collective-permute-start.5) | collective-permute-done | bytes 294944 | tf_op jit(solution)/shard_map/ppermute | solution.py:180
  122.9 0.1 shard_map.76
  123.0 2.4 %collective-permute-start.6 = (s16[2,144,256]{2,1,0:T(8,128)(2,1)S(1)}, s16[2,144,256]{2,1,0:T(8,128)(2,1)S(1)}, u32[]{:S(2)}, u32[]{:S(2)}) collective-permute-start(s16[2,144,256]{2,1,0:T(8,128)(2,1)S(1)} %shard_map.76), channel_id=1, source_target_pairs={{0,6},{1,3},{2,4},{3,1},{4,2},{5,7},{6,0},{7,5},{8,14},{9,11},{10,... | collective-permute-start | bytes 442376 | tf_op jit(solution)/shard_map/ppermute | solution.py:181
  125.4 5.9 %collective-permute-done.6.last = s16[2,144,256]{2,1,0:T(8,128)(2,1)S(1)} collective-permute-done((s16[2,144,256]{2,1,0:T(8,128)(2,1)S(1)}, s16[2,144,256]{2,1,0:T(8,128)(2,1)S(1)}, u32[]{:S(2)}, u32[]{:S(2)}) %collective-permute-start.6) | collective-permute-done | bytes 147488 | tf_op jit(solution)/shard_map/ppermute | solution.py:181
  131.2 0.0 copy-done
  131.2 0.8 shard_map.77
  (1 shorter events, 0.0 us)
Async XLA Ops:
  0.0 104.9 %copy-start.3 = (s32[1,1,1,32]{3,2,1,0:T(1,128)S(1)}, s32[1,1,1,32]{3,2,1,0:T(1,128)}, u32[]{:S(2)}) copy-start(s32[1,1,1,32]{3,2,1,0:T(1,128)} %param.9) | copy-start | bytes 388
  0.0 2.8 %collective-permute-start = (bf16[16,128,128]{2,1,0:T(8,128)(2,1)}, bf16[16,128,128]{2,1,0:T(8,128)(2,1)S(1)}, u32[]{:S(2)}, u32[]{:S(2)}) collective-permute-start(bf16[16,128,128]{2,1,0:T(8,128)(2,1)} %param.8), channel_id=1, source_target_pairs={{9,1},{11,3},{13,5},{15,7},{17,9},{19,11},{21,13},{23,15},{25,17},... | collective-permute-start | bytes 1572872 | tf_op jit(solution)/shard_map/ppermute | solution.py:158
  2.9 98.6 %collective-permute-start.1 = (bf16[32,128,128]{2,1,0:T(8,128)(2,1)S(1)}, bf16[32,128,128]{2,1,0:T(8,128)(2,1)S(1)}, u32[]{:S(2)}, u32[]{:S(2)}) collective-permute-start(bf16[32,128,128]{2,1,0:T(8,128)(2,1)S(1)} %constant_dynamic-update-slice_fusion.near), channel_id=1, source_target_pairs={{17,1},{19,3},{21,5},{23,7},{25,9},{27,11},{29,13},{31,15},{1,17},... | collective-permute-start | bytes 3145736 | tf_op jit(solution)/shard_map/ppermute | solution.py:160
  101.5 6.0 %copy-start.1 = (s32[1,1,1,16,12]{3,2,4,1,0:T(1,128)S(1)}, s32[1,1,1,16,12]{3,2,4,1,0:T(1,128)}, u32[]{:S(2)}) copy-start(s32[1,1,1,16,12]{3,2,4,1,0:T(1,128)} %param.10) | copy-start | bytes 2308
  101.5 6.0 %copy-start.2 = (s32[1,1,1,16,12]{3,2,4,1,0:T(1,128)S(1)}, s32[1,1,1,16,12]{3,2,4,1,0:T(1,128)}, u32[]{:S(2)}) copy-start(s32[1,1,1,16,12]{3,2,4,1,0:T(1,128)} %param.11) | copy-start | bytes 2308
  101.5 5.9 %collective-permute-start.3 = (bf16[32,128,128]{2,1,0:T(8,128)(2,1)S(1)}, bf16[32,128,128]{2,1,0:T(8,128)(2,1)S(1)}, u32[]{:S(2)}, u32[]{:S(2)}) collective-permute-start(bf16[32,128,128]{2,1,0:T(8,128)(2,1)S(1)} %collective-permute-done.1.far), channel_id=1, source_target_pairs={{1,0},{3,2},{5,4},{7,6},{9,8},{11,10},{13,12},{15,14},{17,16},{19,... | collective-permute-start | bytes 3145736 | tf_op jit(solution)/shard_map/ppermute | solution.py:165
  103.6 3.9 %collective-permute-start.2 = (bf16[16,128,128]{2,1,0:T(8,128)(2,1)S(1)}, bf16[16,128,128]{2,1,0:T(8,128)(2,1)S(1)}, u32[]{:S(2)}, u32[]{:S(2)}) collective-permute-start(bf16[16,128,128]{2,1,0:T(8,128)(2,1)S(1)} %collective-permute-done), channel_id=1, source_target_pairs={{1,0},{3,2},{5,4},{7,6},{9,8},{11,10},{13,12},{15,14},{17,16},{19,... | collective-permute-start | bytes 1572872 | tf_op jit(solution)/shard_map/ppermute | solution.py:161
  109.3 21.9 %copy-start = (f32[2,128,256]{2,1,0:T(8,128)S(1)}, f32[2,128,256]{2,1,0:T(8,128)}, u32[]{:S(2)}) copy-start(f32[2,128,256]{2,1,0:T(8,128)} %denominators.1) | copy-start | bytes 786436
  109.3 4.7 %collective-permute-start.4 = (f32[8,128,256]{2,1,0:T(8,128)S(1)}, f32[8,128,256]{2,1,0:T(8,128)S(1)}, u32[]{:S(2)}, u32[]{:S(2)}) collective-permute-start(f32[8,128,256]{2,1,0:T(8,128)S(1)} %shard_map.74), channel_id=1, source_target_pairs={{0,1},{1,0},{2,3},{3,2},{4,5},{5,4},{6,7},{7,6},{8,9},{9,8},{10,11... | collective-permute-start | bytes 3145736 | tf_op jit(solution)/shard_map/ppermute | solution.py:172
  114.2 8.6 %collective-permute-start.5 = (s16[2,2,144,256]{3,2,1,0:T(8,128)(2,1)S(1)}, s16[2,2,144,256]{3,2,1,0:T(8,128)(2,1)S(1)}, u32[]{:S(2)}, u32[]{:S(2)}) collective-permute-start(s16[2,2,144,256]{3,2,1,0:T(8,128)(2,1)S(1)} %get-tuple-element.12), channel_id=1, source_target_pairs={{0,2},{1,7},{2,0},{3,5},{4,6},{5,3},{6,4},{7,1},{8,10},{9,15},{10,... | collective-permute-start | bytes 884744 | tf_op jit(solution)/shard_map/ppermute | solution.py:180
  123.0 8.2 %collective-permute-start.6 = (s16[2,144,256]{2,1,0:T(8,128)(2,1)S(1)}, s16[2,144,256]{2,1,0:T(8,128)(2,1)S(1)}, u32[]{:S(2)}, u32[]{:S(2)}) collective-permute-start(s16[2,144,256]{2,1,0:T(8,128)(2,1)S(1)} %shard_map.76), channel_id=1, source_target_pairs={{0,6},{1,3},{2,4},{3,1},{4,2},{5,7},{6,0},{7,5},{8,14},{9,11},{10,... | collective-permute-start | bytes 442376 | tf_op jit(solution)/shard_map/ppermute | solution.py:181

commit v6 on v5

--- a/solution.py
+++ b/solution.py
@@ -14,6 +14,7 @@
 UNROLL = 2
 TOP = 32760.0
 EXTRA = 16
+ORDER = ((2, 1, 3), (2, 3, 1))
 
 
 def place_here():
@@ -80,10 +81,6 @@
     )(live, slots, ints, *blocks)
 
 
-def partner(chip, core, step):
-    return chip ^ 1 if (core + step) % 2 == 0 else 3 - chip
-
-
 def encode(values, target):
     rows, columns = values.shape
     peak = jnp.maximum(jnp.max(jnp.abs(values), axis=0, keepdims=True), 1e-30)
@@ -99,31 +96,27 @@
     return source[:rows].astype(jnp.int32).astype(jnp.float32) * (jnp.exp2(exponent) * (1 / TOP))
 
 
-def combine(per_chip, mine, came, keep, send):
+def steps_of(core):
+    return ORDER[core]
+
+
+def combine(per_chip, mine, came, keep, *sends):
     place = place_here()
     here, core = lax.div(place, 2), lax.rem(place, 2)
-    near = lax.bitwise_xor(here, 1)
-    first = jnp.where(core == 0, near, 3 - here)
-    second = jnp.where(core == 0, 3 - here, near)
-    across = lax.bitwise_xor(here, 2)
-    for at, block in enumerate((first, across)):
+    for send, zero, one in zip(sends, steps_of(0), steps_of(1)):
+        block = lax.rem(here + jnp.where(core == 0, zero, one), len(sends) + 1)
         for j in range(per_chip):
             t = block * per_chip + j
-            encode(mine[t] + came[t], send.at[at, j])
-    for at, block in enumerate((here, second)):
-        for j in range(per_chip):
-            t = block * per_chip + j
-            keep[at, j] = mine[t] + came[t]
+            encode(mine[t] + came[t], send.at[j])
+    for j in range(per_chip):
+        t = here * per_chip + j
+        keep[j] = mine[t] + came[t]
 
 
-def pass_on(keep, half, send):
-    for j in range(keep.shape[1]):
-        encode(keep[1, j] + decode(half.at[1, j]), send.at[j])
-
-
-def finish(keep, half, last, denominators, out):
-    for j in range(keep.shape[1]):
-        out[j] = (keep[0, j] + decode(half.at[0, j]) + decode(last.at[j])) / denominators[j]
+def finish(keep, first, second, third, denominators, out):
+    for j in range(keep.shape[0]):
+        total = keep[j] + decode(first.at[j]) + decode(second.at[j]) + decode(third.at[j])
+        out[j] = total / denominators[j]
 
 
 def on_chip(kernel, shapes, *arrays):
@@ -172,15 +165,15 @@
     came = lax.ppermute(other, "red", [(k, k ^ 1) for k in range(reds)])
     mine = call_contract(0, per_chip, tiles, *tables)
     rows, columns = mine.shape[1:]
-    whole = jax.ShapeDtypeStruct((2, per_chip, rows, columns), jnp.float32)
-    coded = jax.ShapeDtypeStruct((2, per_chip, rows + EXTRA, columns), jnp.int16)
-    one_coded = jax.ShapeDtypeStruct(coded.shape[1:], jnp.int16)
-    keep, send = on_chip(functools.partial(combine, per_chip), (whole, coded), mine, came)
-    ways = [[(k, 2 * partner(k // 2, k % 2, step) + k % 2) for k in range(reds)] for step in range(2)]
-    half = lax.ppermute(send, "red", ways[0])
-    last = lax.ppermute(on_chip(pass_on, one_coded, keep, half), "red", ways[1])
+    whole = jax.ShapeDtypeStruct((per_chip, rows, columns), jnp.float32)
+    coded = jax.ShapeDtypeStruct((per_chip, rows + EXTRA, columns), jnp.int16)
+    keep, *sends = on_chip(functools.partial(combine, per_chip), (whole, coded, coded, coded), mine, came)
+    parts = [
+        lax.ppermute(send, "red", [(k, (k + 2 * steps_of(k % 2)[i]) % reds) for k in range(reds)])
+        for i, send in enumerate(sends)
+    ]
     return on_chip(
-        finish, jax.ShapeDtypeStruct(denominators.shape, jnp.float32), keep, half, last, denominators
+        finish, jax.ShapeDtypeStruct(denominators.shape, jnp.float32), keep, *parts, denominators
     )
 
 

time: 134 us -> 132 us (0.985)
  waiting for transfers between devices: 13.1 us -> 7.82 us
  starting transfers between devices: 12 us -> 15.5 us
    ppermute x2 -> x3, waiting for transfers between devices: 11.2 us -> 6.32 us  [on_device(): lax.ppermute(send, 'red', [(k, (k + 2 * steps_of(k % 2)[i]) % reds) for k...]
    ppermute x2 -> x3, starting transfers between devices: 5.61 us -> 9.24 us  [on_device(): lax.ppermute(send, 'red', [(k, (k + 2 * steps_of(k % 2)[i]) % reds) for k...]
  transfers between devices with their start and end apart: 7 -> 8, of which waited for: 4 -> 5; matrix products, arithmetic and copies ran while one was open for 3% -> 3% of each run, Pallas kernels for 1% -> 2%
where the time goes in v6:
time: 132 us; the launch traced here: 131 us
  blocking collectives  97.8 us (74%)
  starting transfers between devices  15.5 us (12%)
  waiting for transfers between devices  7.82 us (6%)
  Pallas kernels  5.78 us (4%)
  other arithmetic  2.27 us (2%)
    all_gather x1, blocking collectives, on_device(): every = lax.all_gather(lifted, 'owner', axis=0, tiled=True)  97.8 us
    ppermute x3, starting transfers between devices, on_device(): lax.ppermute(send, 'red', [(k, (k + 2 * steps_of(k % 2)[i]) % reds) for k...  9.24 us
    ppermute x3, waiting for transfers between devices, on_device(): lax.ppermute(send, 'red', [(k, (k + 2 * steps_of(k % 2)[i]) % reds) for k...  6.32 us
    pallas_call x2, Pallas kernels, call_contract(): pl.pallas_call(functools.partial(contract, per_chip, flip), out_shape=jax...  4.67 us
  transfers between devices with their start and end apart: 8, of which 5 were waited for; matrix products, arithmetic and copies ran while one was open for 3% of the time, Pallas kernels for 2%

profile of v6, /device:TPU:6, one launch (start us, length us, event | category | flops | bytes accessed | tf_op | source)
XLA Modules:
  0.0 131.2 jit_solution(8025961620115076838)
XLA Ops:
  0.0 0.0 copy-start.3
  0.0 0.8 collective-permute-start
  0.8 1.1 constant_dynamic-update-slice_fusion.1
  1.9 0.9 multiply_convert_fusion.1
  2.8 0.0 collective-permute-done
  2.9 0.1 constant_dynamic-update-slice_fusion.near
  2.9 0.7 collective-permute-start.1
  3.7 97.8 %all-gather.1 = f16[64,128,256]{2,1,0:T(8,128)(2,1)S(1)} all-gather(f16[2,128,256]{2,1,0:T(8,128)(2,1)S(1)} %multiply_convert_fusion.1), channel_id=1, replica_groups=mesh['owner'=32,'slab'=4,'red'=8] {'owner'}, dimensions={0}, use_global_device_ids=true | all-gather | bytes 4325376 | tf_op jit(solution)/shard_map/all_gather | solution.py:156
  101.5 0.0 copy-start.1
  101.5 0.0 copy-start.2
  101.5 0.0 collective-permute-done.1.far
  101.5 1.4 %collective-permute-start.3 = (bf16[32,128,128]{2,1,0:T(8,128)(2,1)S(1)}, bf16[32,128,128]{2,1,0:T(8,128)(2,1)S(1)}, u32[]{:S(2)}, u32[]{:S(2)}) collective-permute-start(bf16[32,128,128]{2,1,0:T(8,128)(2,1)S(1)} %collective-permute-done.1.far), channel_id=1, source_target_pairs={{1,0},{3,2},{5,4},{7,6},{9,8},{11,10},{13,12},{15,14},{17,16},{19,... | collective-permute-start | bytes 3145736 | tf_op jit(solution)/shard_map/ppermute | solution.py:158
  103.6 1.3 collective-permute-start.2
  104.9 0.0 copy-done.3
  104.9 1.3 %multiply_convert_fusion.pulled = bf16[32,128,256]{2,1,0:T(8,128)(2,1)S(1)} fusion(f16[32,2,128,256]{3,2,1,0:T(8,128)(2,1)S(1)} %bitcast.23, pred[32]{0:T(512)(128)(4,1)S(1)} %compare_bitcast_fusion), kind=kLoop, calls=%fused_computation | loop fusion | flops 4194304 | bytes 6291488 | tf_op jit(solution)/shard_map/convert_element_type | solution.py:161
  106.2 1.2 collective-permute-done.2.next_given
  107.4 0.0 collective-permute-done.3.far_given
  107.4 0.0 copy-done.1
  107.4 0.0 copy-done.2
  107.4 2.3 %shard_map.74 = f32[8,128,256]{2,1,0:T(8,128)S(1)} custom-call(s32[1,1,1]{2,1,0:T(1,128)S(6)} %copy.15.live, s32[1,1,12,1,16]{4,3,2,1,0:T(1,128)S(1)} %bitcast.19, s32[1,1,12,1,16]{4,3,2,1,0:T(1,128)S(1)} %bitcast.21, bf16[32,128,128]{2,1,0:T(8,128)(2,1)S(1)} %constant_dynamic-update-slice_fusion.near, bf16[32,128,128]{2,1,0:T(8,128)(2,1)S(1)} %collective-permute-done.1.far, ...), custom_call_target="tpu_custom_call" | custom-call | flops 805306368 | bytes 1048576 | tf_op jit(solution)/shard_map/pallas_call | solution.py:70
  109.8 0.0 copy-start
  109.8 2.1 %collective-permute-start.4 = (f32[8,128,256]{2,1,0:T(8,128)S(1)}, f32[8,128,256]{2,1,0:T(8,128)S(1)}, u32[]{:S(2)}, u32[]{:S(2)}) collective-permute-start(f32[8,128,256]{2,1,0:T(8,128)S(1)} %shard_map.74), channel_id=1, source_target_pairs={{0,1},{1,0},{2,3},{3,2},{4,5},{5,4},{6,7},{7,6},{8,9},{9,8},{10,11... | collective-permute-start | bytes 3145736 | tf_op jit(solution)/shard_map/ppermute | solution.py:165
  111.9 2.3 %shard_map.73.mine = f32[8,128,256]{2,1,0:T(8,128)S(1)} custom-call(s32[1,1,1]{2,1,0:T(1,128)S(6)} %copy.15.live, s32[1,1,12,1,16]{4,3,2,1,0:T(1,128)S(1)} %bitcast.20, s32[1,1,12,1,16]{4,3,2,1,0:T(1,128)S(1)} %bitcast.22, bf16[32,128,128]{2,1,0:T(8,128)(2,1)S(1)} %constant_dynamic-update-slice_fusion.near, ...), custom_call_target="tpu_custom_call" | custom-call | flops 805306368 | bytes 1048576 | tf_op jit(solution)/shard_map/pallas_call | solution.py:70
  114.2 0.3 collective-permute-done.4.came
  114.5 0.3 shard_map.75
  114.8 2.8 %collective-permute-start.5 = (s16[2,144,256]{2,1,0:T(8,128)(2,1)S(1)}, s16[2,144,256]{2,1,0:T(8,128)(2,1)S(1)}, u32[]{:S(2)}, u32[]{:S(2)}) collective-permute-start(s16[2,144,256]{2,1,0:T(8,128)(2,1)S(1)} %get-tuple-element.14), channel_id=1, source_target_pairs={{0,4},{1,5},{2,6},{3,7},{4,0},{5,1},{6,2},{7,3},{8,12},{9,13},{10,... | collective-permute-start | bytes 442376 | tf_op jit(solution)/shard_map/ppermute | solution.py:172
  117.6 4.5 %collective-permute-start.6 = (s16[2,144,256]{2,1,0:T(8,128)(2,1)S(1)}, s16[2,144,256]{2,1,0:T(8,128)(2,1)S(1)}, u32[]{:S(2)}, u32[]{:S(2)}) collective-permute-start(s16[2,144,256]{2,1,0:T(8,128)(2,1)S(1)} %get-tuple-element.15), channel_id=1, source_target_pairs={{0,2},{1,7},{2,4},{3,1},{4,6},{5,3},{6,0},{7,5},{8,10},{9,15},{10,... | collective-permute-start | bytes 442376 | tf_op jit(solution)/shard_map/ppermute | solution.py:172
  122.1 1.9 %collective-permute-start.7 = (s16[2,144,256]{2,1,0:T(8,128)(2,1)S(1)}, s16[2,144,256]{2,1,0:T(8,128)(2,1)S(1)}, u32[]{:S(2)}, u32[]{:S(2)}) collective-permute-start(s16[2,144,256]{2,1,0:T(8,128)(2,1)S(1)} %get-tuple-element.16), channel_id=1, source_target_pairs={{0,6},{1,3},{2,0},{3,5},{4,2},{5,7},{6,4},{7,1},{8,14},{9,11},{10,... | collective-permute-start | bytes 442376 | tf_op jit(solution)/shard_map/ppermute | solution.py:172
  124.0 0.1 collective-permute-done.5.first
  124.1 1.0 collective-permute-done.6.second
  125.1 5.2 %collective-permute-done.7.third = s16[2,144,256]{2,1,0:T(8,128)(2,1)S(1)} collective-permute-done((s16[2,144,256]{2,1,0:T(8,128)(2,1)S(1)}, s16[2,144,256]{2,1,0:T(8,128)(2,1)S(1)}, u32[]{:S(2)}, u32[]{:S(2)}) %collective-permute-start.7) | collective-permute-done | bytes 147488 | tf_op jit(solution)/shard_map/ppermute | solution.py:172
  130.3 0.0 copy-done
  130.4 0.8 shard_map.76
  (1 shorter events, 0.0 us)
Async XLA Ops:
  0.0 104.9 %copy-start.3 = (s32[1,1,1,32]{3,2,1,0:T(1,128)S(1)}, s32[1,1,1,32]{3,2,1,0:T(1,128)}, u32[]{:S(2)}) copy-start(s32[1,1,1,32]{3,2,1,0:T(1,128)} %param.9) | copy-start | bytes 388
  0.0 2.8 %collective-permute-start = (bf16[16,128,128]{2,1,0:T(8,128)(2,1)}, bf16[16,128,128]{2,1,0:T(8,128)(2,1)S(1)}, u32[]{:S(2)}, u32[]{:S(2)}) collective-permute-start(bf16[16,128,128]{2,1,0:T(8,128)(2,1)} %param.8), channel_id=1, source_target_pairs={{9,1},{11,3},{13,5},{15,7},{17,9},{19,11},{21,13},{23,15},{25,17},... | collective-permute-start | bytes 1572872 | tf_op jit(solution)/shard_map/ppermute | solution.py:151
  2.9 98.6 %collective-permute-start.1 = (bf16[32,128,128]{2,1,0:T(8,128)(2,1)S(1)}, bf16[32,128,128]{2,1,0:T(8,128)(2,1)S(1)}, u32[]{:S(2)}, u32[]{:S(2)}) collective-permute-start(bf16[32,128,128]{2,1,0:T(8,128)(2,1)S(1)} %constant_dynamic-update-slice_fusion.near), channel_id=1, source_target_pairs={{17,1},{19,3},{21,5},{23,7},{25,9},{27,11},{29,13},{31,15},{1,17},... | collective-permute-start | bytes 3145736 | tf_op jit(solution)/shard_map/ppermute | solution.py:153
  101.5 6.0 %copy-start.1 = (s32[1,1,1,16,12]{3,2,4,1,0:T(1,128)S(1)}, s32[1,1,1,16,12]{3,2,4,1,0:T(1,128)}, u32[]{:S(2)}) copy-start(s32[1,1,1,16,12]{3,2,4,1,0:T(1,128)} %param.10) | copy-start | bytes 2308
  101.5 6.0 %copy-start.2 = (s32[1,1,1,16,12]{3,2,4,1,0:T(1,128)S(1)}, s32[1,1,1,16,12]{3,2,4,1,0:T(1,128)}, u32[]{:S(2)}) copy-start(s32[1,1,1,16,12]{3,2,4,1,0:T(1,128)} %param.11) | copy-start | bytes 2308
  101.5 5.9 %collective-permute-start.3 = (bf16[32,128,128]{2,1,0:T(8,128)(2,1)S(1)}, bf16[32,128,128]{2,1,0:T(8,128)(2,1)S(1)}, u32[]{:S(2)}, u32[]{:S(2)}) collective-permute-start(bf16[32,128,128]{2,1,0:T(8,128)(2,1)S(1)} %collective-permute-done.1.far), channel_id=1, source_target_pairs={{1,0},{3,2},{5,4},{7,6},{9,8},{11,10},{13,12},{15,14},{17,16},{19,... | collective-permute-start | bytes 3145736 | tf_op jit(solution)/shard_map/ppermute | solution.py:158
  103.6 3.9 %collective-permute-start.2 = (bf16[16,128,128]{2,1,0:T(8,128)(2,1)S(1)}, bf16[16,128,128]{2,1,0:T(8,128)(2,1)S(1)}, u32[]{:S(2)}, u32[]{:S(2)}) collective-permute-start(bf16[16,128,128]{2,1,0:T(8,128)(2,1)S(1)} %collective-permute-done), channel_id=1, source_target_pairs={{1,0},{3,2},{5,4},{7,6},{9,8},{11,10},{13,12},{15,14},{17,16},{19,... | collective-permute-start | bytes 1572872 | tf_op jit(solution)/shard_map/ppermute | solution.py:154
  109.8 20.6 %copy-start = (f32[2,128,256]{2,1,0:T(8,128)S(1)}, f32[2,128,256]{2,1,0:T(8,128)}, u32[]{:S(2)}) copy-start(f32[2,128,256]{2,1,0:T(8,128)} %denominators.1) | copy-start | bytes 786436
  109.8 4.7 %collective-permute-start.4 = (f32[8,128,256]{2,1,0:T(8,128)S(1)}, f32[8,128,256]{2,1,0:T(8,128)S(1)}, u32[]{:S(2)}, u32[]{:S(2)}) collective-permute-start(f32[8,128,256]{2,1,0:T(8,128)S(1)} %shard_map.74), channel_id=1, source_target_pairs={{0,1},{1,0},{2,3},{3,2},{4,5},{5,4},{6,7},{7,6},{8,9},{9,8},{10,11... | collective-permute-start | bytes 3145736 | tf_op jit(solution)/shard_map/ppermute | solution.py:165
  114.8 9.4 %collective-permute-start.5 = (s16[2,144,256]{2,1,0:T(8,128)(2,1)S(1)}, s16[2,144,256]{2,1,0:T(8,128)(2,1)S(1)}, u32[]{:S(2)}, u32[]{:S(2)}) collective-permute-start(s16[2,144,256]{2,1,0:T(8,128)(2,1)S(1)} %get-tuple-element.14), channel_id=1, source_target_pairs={{0,4},{1,5},{2,6},{3,7},{4,0},{5,1},{6,2},{7,3},{8,12},{9,13},{10,... | collective-permute-start | bytes 442376 | tf_op jit(solution)/shard_map/ppermute | solution.py:172
  117.6 7.5 %collective-permute-start.6 = (s16[2,144,256]{2,1,0:T(8,128)(2,1)S(1)}, s16[2,144,256]{2,1,0:T(8,128)(2,1)S(1)}, u32[]{:S(2)}, u32[]{:S(2)}) collective-permute-start(s16[2,144,256]{2,1,0:T(8,128)(2,1)S(1)} %get-tuple-element.15), channel_id=1, source_target_pairs={{0,2},{1,7},{2,4},{3,1},{4,6},{5,3},{6,0},{7,5},{8,10},{9,15},{10,... | collective-permute-start | bytes 442376 | tf_op jit(solution)/shard_map/ppermute | solution.py:172
  122.1 8.2 %collective-permute-start.7 = (s16[2,144,256]{2,1,0:T(8,128)(2,1)S(1)}, s16[2,144,256]{2,1,0:T(8,128)(2,1)S(1)}, u32[]{:S(2)}, u32[]{:S(2)}) collective-permute-start(s16[2,144,256]{2,1,0:T(8,128)(2,1)S(1)} %get-tuple-element.16), channel_id=1, source_target_pairs={{0,6},{1,3},{2,0},{3,5},{4,2},{5,7},{6,4},{7,1},{8,14},{9,11},{10,... | collective-permute-start | bytes 442376 | tf_op jit(solution)/shard_map/ppermute | solution.py:172

commit v7 on v6

--- a/solution.py
+++ b/solution.py
@@ -11,7 +11,7 @@
 SMEM = pltpu.SMEM
 LIFT = 2.0**13
 WIDTH = 4
-UNROLL = 2
+UNROLL = 4
 TOP = 32760.0
 EXTRA = 16
 ORDER = ((2, 1, 3), (2, 3, 1))
@@ -154,7 +154,7 @@
     next_given = lax.ppermute(beyond, "red", give)
     lifted = (amplitudes * jnp.asarray(LIFT, amplitudes.dtype)).astype(jnp.float16)
     every = lax.all_gather(lifted, "owner", axis=0, tiled=True)
-    every, far = lax.optimization_barrier((every, far))
+    every, far, next_given = lax.optimization_barrier((every, far, next_given))
     far_given = lax.ppermute(far, "red", give)
     every = every.reshape(owners, -1, *every.shape[1:])
     pulled = jnp.where((wanted == 0)[:, None, None], every[:, 0], every[:, 1])

time: 132 us -> 132 us (level)
  transfers between devices with their start and end apart: 8 -> 8, of which waited for: 5 -> 4; matrix products, arithmetic and copies ran while one was open for 3% -> 3% of each run, Pallas kernels for 2% -> 2%
where the time goes in v7:
time: 132 us
  blocking collectives  98.1 us (74%)
  starting transfers between devices  16.3 us (12%)
  waiting for transfers between devices  7.79 us (6%)
  Pallas kernels  5.25 us (4%)
  other arithmetic  2.27 us (2%)
    all_gather x1, blocking collectives, on_device(): every = lax.all_gather(lifted, 'owner', axis=0, tiled=True)  98.1 us
    ppermute x3, starting transfers between devices, on_device(): lax.ppermute(send, 'red', [(k, (k + 2 * steps_of(k % 2)[i]) % reds) for k...  9.66 us
    ppermute x3, waiting for transfers between devices, on_device(): lax.ppermute(send, 'red', [(k, (k + 2 * steps_of(k % 2)[i]) % reds) for k...  6.31 us
    pallas_call x2, Pallas kernels, call_contract(): pl.pallas_call(functools.partial(contract, per_chip, flip), out_shape=jax...  4.14 us
  transfers between devices with their start and end apart: 8, of which 4 were waited for; matrix products, arithmetic and copies ran while one was open for 3% of the time, Pallas kernels for 2%

profile of v7, /device:TPU:6, one launch (start us, length us, event | category | flops | bytes accessed | tf_op | source)
XLA Modules:
  0.0 131.6 jit_solution(10077575722861966617)
XLA Ops:
  0.0 0.0 copy-start.3
  0.0 0.8 collective-permute-start
  0.8 1.1 constant_dynamic-update-slice_fusion.1
  1.9 0.9 multiply_convert_fusion.1
  2.8 0.0 collective-permute-done
  2.9 0.1 constant_dynamic-update-slice_fusion.near
  2.9 0.7 collective-permute-start.1
  3.7 1.3 collective-permute-start.2
  5.0 98.1 %all-gather.1 = f16[64,128,256]{2,1,0:T(8,128)(2,1)S(1)} all-gather(f16[2,128,256]{2,1,0:T(8,128)(2,1)S(1)} %multiply_convert_fusion.1), channel_id=1, replica_groups=mesh['owner'=32,'slab'=4,'red'=8] {'owner'}, dimensions={0}, use_global_device_ids=true | all-gather | bytes 4325376 | tf_op jit(solution)/shard_map/all_gather | solution.py:156
  103.0 0.0 copy-start.1
  103.0 0.0 copy-start.2
  103.0 0.0 collective-permute-done.2.next_given
  103.0 0.0 collective-permute-done.1.far
  103.0 1.4 %collective-permute-start.3 = (bf16[32,128,128]{2,1,0:T(8,128)(2,1)S(1)}, bf16[32,128,128]{2,1,0:T(8,128)(2,1)S(1)}, u32[]{:S(2)}, u32[]{:S(2)}) collective-permute-start(bf16[32,128,128]{2,1,0:T(8,128)(2,1)S(1)} %collective-permute-done.1.far), channel_id=1, source_target_pairs={{1,0},{3,2},{5,4},{7,6},{9,8},{11,10},{13,12},{15,14},{17,16},{19,... | collective-permute-start | bytes 3145736 | tf_op jit(solution)/shard_map/ppermute | solution.py:158
  105.1 0.0 copy-done.3
  105.1 1.3 %multiply_convert_fusion.pulled = bf16[32,128,256]{2,1,0:T(8,128)(2,1)S(1)} fusion(f16[32,2,128,256]{3,2,1,0:T(8,128)(2,1)S(1)} %bitcast.23, pred[32]{0:T(512)(128)(4,1)S(1)} %compare_bitcast_fusion), kind=kLoop, calls=%fused_computation | loop fusion | flops 4194304 | bytes 6291488 | tf_op jit(solution)/shard_map/convert_element_type | solution.py:161
  106.5 1.2 collective-permute-done.3.far_given
  107.7 0.0 copy-done.1
  107.7 0.0 copy-done.2
  107.7 2.1 %shard_map.74 = f32[8,128,256]{2,1,0:T(8,128)S(1)} custom-call(s32[1,1,1]{2,1,0:T(1,128)S(6)} %copy.15.live, s32[1,1,12,1,16]{4,3,2,1,0:T(1,128)S(1)} %bitcast.19, s32[1,1,12,1,16]{4,3,2,1,0:T(1,128)S(1)} %bitcast.21, bf16[32,128,128]{2,1,0:T(8,128)(2,1)S(1)} %constant_dynamic-update-slice_fusion.near, bf16[32,128,128]{2,1,0:T(8,128)(2,1)S(1)} %collective-permute-done.1.far, ...), custom_call_target="tpu_custom_call" | custom-call | flops 805306368 | bytes 1048576 | tf_op jit(solution)/shard_map/pallas_call | solution.py:70
  109.8 0.0 copy-start
  109.8 2.4 %collective-permute-start.4 = (f32[8,128,256]{2,1,0:T(8,128)S(1)}, f32[8,128,256]{2,1,0:T(8,128)S(1)}, u32[]{:S(2)}, u32[]{:S(2)}) collective-permute-start(f32[8,128,256]{2,1,0:T(8,128)S(1)} %shard_map.74), channel_id=1, source_target_pairs={{0,1},{1,0},{2,3},{3,2},{4,5},{5,4},{6,7},{7,6},{8,9},{9,8},{10,11... | collective-permute-start | bytes 3145736 | tf_op jit(solution)/shard_map/ppermute | solution.py:165
  112.2 2.1 %shard_map.73.mine = f32[8,128,256]{2,1,0:T(8,128)S(1)} custom-call(s32[1,1,1]{2,1,0:T(1,128)S(6)} %copy.15.live, s32[1,1,12,1,16]{4,3,2,1,0:T(1,128)S(1)} %bitcast.20, s32[1,1,12,1,16]{4,3,2,1,0:T(1,128)S(1)} %bitcast.22, bf16[32,128,128]{2,1,0:T(8,128)(2,1)S(1)} %constant_dynamic-update-slice_fusion.near, ...), custom_call_target="tpu_custom_call" | custom-call | flops 805306368 | bytes 1048576 | tf_op jit(solution)/shard_map/pallas_call | solution.py:70
  114.3 0.2 collective-permute-done.4.came
  114.5 0.3 shard_map.75
  114.8 3.3 %collective-permute-start.5 = (s16[2,144,256]{2,1,0:T(8,128)(2,1)S(1)}, s16[2,144,256]{2,1,0:T(8,128)(2,1)S(1)}, u32[]{:S(2)}, u32[]{:S(2)}) collective-permute-start(s16[2,144,256]{2,1,0:T(8,128)(2,1)S(1)} %get-tuple-element.16), channel_id=1, source_target_pairs={{0,4},{1,5},{2,6},{3,7},{4,0},{5,1},{6,2},{7,3},{8,12},{9,13},{10,... | collective-permute-start | bytes 442376 | tf_op jit(solution)/shard_map/ppermute | solution.py:172
  118.1 4.4 %collective-permute-start.6 = (s16[2,144,256]{2,1,0:T(8,128)(2,1)S(1)}, s16[2,144,256]{2,1,0:T(8,128)(2,1)S(1)}, u32[]{:S(2)}, u32[]{:S(2)}) collective-permute-start(s16[2,144,256]{2,1,0:T(8,128)(2,1)S(1)} %get-tuple-element.17), channel_id=1, source_target_pairs={{0,2},{1,7},{2,4},{3,1},{4,6},{5,3},{6,0},{7,5},{8,10},{9,15},{10,... | collective-permute-start | bytes 442376 | tf_op jit(solution)/shard_map/ppermute | solution.py:172
  122.5 1.9 %collective-permute-start.7 = (s16[2,144,256]{2,1,0:T(8,128)(2,1)S(1)}, s16[2,144,256]{2,1,0:T(8,128)(2,1)S(1)}, u32[]{:S(2)}, u32[]{:S(2)}) collective-permute-start(s16[2,144,256]{2,1,0:T(8,128)(2,1)S(1)} %get-tuple-element.18), channel_id=1, source_target_pairs={{0,6},{1,3},{2,0},{3,5},{4,2},{5,7},{6,4},{7,1},{8,14},{9,11},{10,... | collective-permute-start | bytes 442376 | tf_op jit(solution)/shard_map/ppermute | solution.py:172
  124.5 0.0 collective-permute-done.5.first
  124.5 1.2 collective-permute-done.6.second
  125.7 5.1 %collective-permute-done.7.third = s16[2,144,256]{2,1,0:T(8,128)(2,1)S(1)} collective-permute-done((s16[2,144,256]{2,1,0:T(8,128)(2,1)S(1)}, s16[2,144,256]{2,1,0:T(8,128)(2,1)S(1)}, u32[]{:S(2)}, u32[]{:S(2)}) %collective-permute-start.7) | collective-permute-done | bytes 147488 | tf_op jit(solution)/shard_map/ppermute | solution.py:172
  130.8 0.0 copy-done
  130.8 0.8 shard_map.76
  (1 shorter events, 0.0 us)
Async XLA Ops:
  0.0 105.1 %copy-start.3 = (s32[1,1,1,32]{3,2,1,0:T(1,128)S(1)}, s32[1,1,1,32]{3,2,1,0:T(1,128)}, u32[]{:S(2)}) copy-start(s32[1,1,1,32]{3,2,1,0:T(1,128)} %param.9) | copy-start | bytes 388
  0.0 2.8 %collective-permute-start = (bf16[16,128,128]{2,1,0:T(8,128)(2,1)}, bf16[16,128,128]{2,1,0:T(8,128)(2,1)S(1)}, u32[]{:S(2)}, u32[]{:S(2)}) collective-permute-start(bf16[16,128,128]{2,1,0:T(8,128)(2,1)} %param.8), channel_id=1, source_target_pairs={{9,1},{11,3},{13,5},{15,7},{17,9},{19,11},{21,13},{23,15},{25,17},... | collective-permute-start | bytes 1572872 | tf_op jit(solution)/shard_map/ppermute | solution.py:151
  2.9 100.1 %collective-permute-start.1 = (bf16[32,128,128]{2,1,0:T(8,128)(2,1)S(1)}, bf16[32,128,128]{2,1,0:T(8,128)(2,1)S(1)}, u32[]{:S(2)}, u32[]{:S(2)}) collective-permute-start(bf16[32,128,128]{2,1,0:T(8,128)(2,1)S(1)} %constant_dynamic-update-slice_fusion.near), channel_id=1, source_target_pairs={{17,1},{19,3},{21,5},{23,7},{25,9},{27,11},{29,13},{31,15},{1,17},... | collective-permute-start | bytes 3145736 | tf_op jit(solution)/shard_map/ppermute | solution.py:153
  3.7 99.4 %collective-permute-start.2 = (bf16[16,128,128]{2,1,0:T(8,128)(2,1)S(1)}, bf16[16,128,128]{2,1,0:T(8,128)(2,1)S(1)}, u32[]{:S(2)}, u32[]{:S(2)}) collective-permute-start(bf16[16,128,128]{2,1,0:T(8,128)(2,1)S(1)} %collective-permute-done), channel_id=1, source_target_pairs={{1,0},{3,2},{5,4},{7,6},{9,8},{11,10},{13,12},{15,14},{17,16},{19,... | collective-permute-start | bytes 1572872 | tf_op jit(solution)/shard_map/ppermute | solution.py:154
  103.0 4.7 %copy-start.1 = (s32[1,1,1,16,12]{3,2,4,1,0:T(1,128)S(1)}, s32[1,1,1,16,12]{3,2,4,1,0:T(1,128)}, u32[]{:S(2)}) copy-start(s32[1,1,1,16,12]{3,2,4,1,0:T(1,128)} %param.10) | copy-start | bytes 2308
  103.0 4.7 %copy-start.2 = (s32[1,1,1,16,12]{3,2,4,1,0:T(1,128)S(1)}, s32[1,1,1,16,12]{3,2,4,1,0:T(1,128)}, u32[]{:S(2)}) copy-start(s32[1,1,1,16,12]{3,2,4,1,0:T(1,128)} %param.11) | copy-start | bytes 2308
  103.0 4.7 %collective-permute-start.3 = (bf16[32,128,128]{2,1,0:T(8,128)(2,1)S(1)}, bf16[32,128,128]{2,1,0:T(8,128)(2,1)S(1)}, u32[]{:S(2)}, u32[]{:S(2)}) collective-permute-start(bf16[32,128,128]{2,1,0:T(8,128)(2,1)S(1)} %collective-permute-done.1.far), channel_id=1, source_target_pairs={{1,0},{3,2},{5,4},{7,6},{9,8},{11,10},{13,12},{15,14},{17,16},{19,... | collective-permute-start | bytes 3145736 | tf_op jit(solution)/shard_map/ppermute | solution.py:158
  109.8 21.0 %copy-start = (f32[2,128,256]{2,1,0:T(8,128)S(1)}, f32[2,128,256]{2,1,0:T(8,128)}, u32[]{:S(2)}) copy-start(f32[2,128,256]{2,1,0:T(8,128)} %denominators.1) | copy-start | bytes 786436
  109.8 4.7 %collective-permute-start.4 = (f32[8,128,256]{2,1,0:T(8,128)S(1)}, f32[8,128,256]{2,1,0:T(8,128)S(1)}, u32[]{:S(2)}, u32[]{:S(2)}) collective-permute-start(f32[8,128,256]{2,1,0:T(8,128)S(1)} %shard_map.74), channel_id=1, source_target_pairs={{0,1},{1,0},{2,3},{3,2},{4,5},{5,4},{6,7},{7,6},{8,9},{9,8},{10,11... | collective-permute-start | bytes 3145736 | tf_op jit(solution)/shard_map/ppermute | solution.py:165
  114.8 9.7 %collective-permute-start.5 = (s16[2,144,256]{2,1,0:T(8,128)(2,1)S(1)}, s16[2,144,256]{2,1,0:T(8,128)(2,1)S(1)}, u32[]{:S(2)}, u32[]{:S(2)}) collective-permute-start(s16[2,144,256]{2,1,0:T(8,128)(2,1)S(1)} %get-tuple-element.16), channel_id=1, source_target_pairs={{0,4},{1,5},{2,6},{3,7},{4,0},{5,1},{6,2},{7,3},{8,12},{9,13},{10,... | collective-permute-start | bytes 442376 | tf_op jit(solution)/shard_map/ppermute | solution.py:172
  118.1 7.5 %collective-permute-start.6 = (s16[2,144,256]{2,1,0:T(8,128)(2,1)S(1)}, s16[2,144,256]{2,1,0:T(8,128)(2,1)S(1)}, u32[]{:S(2)}, u32[]{:S(2)}) collective-permute-start(s16[2,144,256]{2,1,0:T(8,128)(2,1)S(1)} %get-tuple-element.17), channel_id=1, source_target_pairs={{0,2},{1,7},{2,4},{3,1},{4,6},{5,3},{6,0},{7,5},{8,10},{9,15},{10,... | collective-permute-start | bytes 442376 | tf_op jit(solution)/shard_map/ppermute | solution.py:172
  122.5 8.2 %collective-permute-start.7 = (s16[2,144,256]{2,1,0:T(8,128)(2,1)S(1)}, s16[2,144,256]{2,1,0:T(8,128)(2,1)S(1)}, u32[]{:S(2)}, u32[]{:S(2)}) collective-permute-start(s16[2,144,256]{2,1,0:T(8,128)(2,1)S(1)} %get-tuple-element.18), channel_id=1, source_target_pairs={{0,6},{1,3},{2,0},{3,5},{4,2},{5,7},{6,4},{7,1},{8,14},{9,11},{10,... | collective-permute-start | bytes 442376 | tf_op jit(solution)/shard_map/ppermute | solution.py:172

commit v8 on v7

--- a/solution.py
+++ b/solution.py
@@ -11,7 +11,7 @@
 SMEM = pltpu.SMEM
 LIFT = 2.0**13
 WIDTH = 4
-UNROLL = 4
+UNROLL = 8
 TOP = 32760.0
 EXTRA = 16
 ORDER = ((2, 1, 3), (2, 3, 1))

time: 132 us -> 132 us (level)
  transfers between devices with their start and end apart: 8 -> 8, of which waited for: 4 -> 5; matrix products, arithmetic and copies ran while one was open for 3% -> 3% of each run, Pallas kernels for 2% -> 2%
where the time goes in v8:
time: 132 us; the launch traced here: 131 us
  blocking collectives  98.1 us (74%)
  starting transfers between devices  15.5 us (12%)
  waiting for transfers between devices  7.69 us (6%)
  Pallas kernels  5.11 us (4%)
  other arithmetic  2.27 us (2%)
    all_gather x1, blocking collectives, on_device(): every = lax.all_gather(lifted, 'owner', axis=0, tiled=True)  98.1 us
    ppermute x3, starting transfers between devices, on_device(): lax.ppermute(send, 'red', [(k, (k + 2 * steps_of(k % 2)[i]) % reds) for k...  9.16 us
    ppermute x3, waiting for transfers between devices, on_device(): lax.ppermute(send, 'red', [(k, (k + 2 * steps_of(k % 2)[i]) % reds) for k...  5.92 us
    pallas_call x2, Pallas kernels, call_contract(): pl.pallas_call(functools.partial(contract, per_chip, flip), out_shape=jax...  4 us
  transfers between devices with their start and end apart: 8, of which 5 were waited for; matrix products, arithmetic and copies ran while one was open for 3% of the time, Pallas kernels for 2%

profile of v8, /device:TPU:6, one launch (start us, length us, event | category | flops | bytes accessed | tf_op | source)
XLA Modules:
  0.0 130.6 jit_solution(8264671918155158039)
XLA Ops:
  0.0 0.0 copy-start.3
  0.0 0.8 collective-permute-start
  0.8 1.1 constant_dynamic-update-slice_fusion.1
  1.9 0.9 multiply_convert_fusion.1
  2.8 0.0 collective-permute-done
  2.9 0.1 constant_dynamic-update-slice_fusion.near
  2.9 0.7 collective-permute-start.1
  3.7 1.3 collective-permute-start.2
  5.0 98.1 %all-gather.1 = f16[64,128,256]{2,1,0:T(8,128)(2,1)S(1)} all-gather(f16[2,128,256]{2,1,0:T(8,128)(2,1)S(1)} %multiply_convert_fusion.1), channel_id=1, replica_groups=mesh['owner'=32,'slab'=4,'red'=8] {'owner'}, dimensions={0}, use_global_device_ids=true | all-gather | bytes 4325376 | tf_op jit(solution)/shard_map/all_gather | solution.py:156
  103.0 0.0 copy-start.1
  103.0 0.0 copy-start.2
  103.0 0.0 collective-permute-done.2.next_given
  103.0 0.0 collective-permute-done.1.far
  103.0 1.4 %collective-permute-start.3 = (bf16[32,128,128]{2,1,0:T(8,128)(2,1)S(1)}, bf16[32,128,128]{2,1,0:T(8,128)(2,1)S(1)}, u32[]{:S(2)}, u32[]{:S(2)}) collective-permute-start(bf16[32,128,128]{2,1,0:T(8,128)(2,1)S(1)} %collective-permute-done.1.far), channel_id=1, source_target_pairs={{1,0},{3,2},{5,4},{7,6},{9,8},{11,10},{13,12},{15,14},{17,16},{19,... | collective-permute-start | bytes 3145736 | tf_op jit(solution)/shard_map/ppermute | solution.py:158
  105.1 0.0 copy-done.3
  105.1 1.3 %multiply_convert_fusion.pulled = bf16[32,128,256]{2,1,0:T(8,128)(2,1)S(1)} fusion(f16[32,2,128,256]{3,2,1,0:T(8,128)(2,1)S(1)} %bitcast.23, pred[32]{0:T(512)(128)(4,1)S(1)} %compare_bitcast_fusion), kind=kLoop, calls=%fused_computation | loop fusion | flops 4194304 | bytes 6291488 | tf_op jit(solution)/shard_map/convert_element_type | solution.py:161
  106.5 1.2 collective-permute-done.3.far_given
  107.7 0.0 copy-done.1
  107.7 0.0 copy-done.2
  107.7 1.9 %shard_map.74 = f32[8,128,256]{2,1,0:T(8,128)S(1)} custom-call(s32[1,1,1]{2,1,0:T(1,128)S(6)} %copy.15.live, s32[1,1,12,1,16]{4,3,2,1,0:T(1,128)S(1)} %bitcast.19, s32[1,1,12,1,16]{4,3,2,1,0:T(1,128)S(1)} %bitcast.21, bf16[32,128,128]{2,1,0:T(8,128)(2,1)S(1)} %constant_dynamic-update-slice_fusion.near, bf16[32,128,128]{2,1,0:T(8,128)(2,1)S(1)} %collective-permute-done.1.far, ...), custom_call_target="tpu_custom_call" | custom-call | flops 805306368 | bytes 1048576 | tf_op jit(solution)/shard_map/pallas_call | solution.py:70
  109.6 0.0 copy-start
  109.7 2.1 %collective-permute-start.4 = (f32[8,128,256]{2,1,0:T(8,128)S(1)}, f32[8,128,256]{2,1,0:T(8,128)S(1)}, u32[]{:S(2)}, u32[]{:S(2)}) collective-permute-start(f32[8,128,256]{2,1,0:T(8,128)S(1)} %shard_map.74), channel_id=1, source_target_pairs={{0,1},{1,0},{2,3},{3,2},{4,5},{5,4},{6,7},{7,6},{8,9},{9,8},{10,11... | collective-permute-start | bytes 3145736 | tf_op jit(solution)/shard_map/ppermute | solution.py:165
  111.7 2.1 %shard_map.73.mine = f32[8,128,256]{2,1,0:T(8,128)S(1)} custom-call(s32[1,1,1]{2,1,0:T(1,128)S(6)} %copy.15.live, s32[1,1,12,1,16]{4,3,2,1,0:T(1,128)S(1)} %bitcast.20, s32[1,1,12,1,16]{4,3,2,1,0:T(1,128)S(1)} %bitcast.22, bf16[32,128,128]{2,1,0:T(8,128)(2,1)S(1)} %constant_dynamic-update-slice_fusion.near, ...), custom_call_target="tpu_custom_call" | custom-call | flops 805306368 | bytes 1048576 | tf_op jit(solution)/shard_map/pallas_call | solution.py:70
  113.8 0.5 collective-permute-done.4.came
  114.3 0.3 shard_map.75
  114.6 3.3 %collective-permute-start.5 = (s16[2,144,256]{2,1,0:T(8,128)(2,1)S(1)}, s16[2,144,256]{2,1,0:T(8,128)(2,1)S(1)}, u32[]{:S(2)}, u32[]{:S(2)}) collective-permute-start(s16[2,144,256]{2,1,0:T(8,128)(2,1)S(1)} %get-tuple-element.16), channel_id=1, source_target_pairs={{0,4},{1,5},{2,6},{3,7},{4,0},{5,1},{6,2},{7,3},{8,12},{9,13},{10,... | collective-permute-start | bytes 442376 | tf_op jit(solution)/shard_map/ppermute | solution.py:172
  117.9 3.5 %collective-permute-start.6 = (s16[2,144,256]{2,1,0:T(8,128)(2,1)S(1)}, s16[2,144,256]{2,1,0:T(8,128)(2,1)S(1)}, u32[]{:S(2)}, u32[]{:S(2)}) collective-permute-start(s16[2,144,256]{2,1,0:T(8,128)(2,1)S(1)} %get-tuple-element.17), channel_id=1, source_target_pairs={{0,2},{1,7},{2,4},{3,1},{4,6},{5,3},{6,0},{7,5},{8,10},{9,15},{10,... | collective-permute-start | bytes 442376 | tf_op jit(solution)/shard_map/ppermute | solution.py:172
  121.5 2.3 %collective-permute-start.7 = (s16[2,144,256]{2,1,0:T(8,128)(2,1)S(1)}, s16[2,144,256]{2,1,0:T(8,128)(2,1)S(1)}, u32[]{:S(2)}, u32[]{:S(2)}) collective-permute-start(s16[2,144,256]{2,1,0:T(8,128)(2,1)S(1)} %get-tuple-element.18), channel_id=1, source_target_pairs={{0,6},{1,3},{2,0},{3,5},{4,2},{5,7},{6,4},{7,1},{8,14},{9,11},{10,... | collective-permute-start | bytes 442376 | tf_op jit(solution)/shard_map/ppermute | solution.py:172
  123.8 0.6 collective-permute-done.5.first
  124.4 1.1 collective-permute-done.6.second
  125.6 4.2 %collective-permute-done.7.third = s16[2,144,256]{2,1,0:T(8,128)(2,1)S(1)} collective-permute-done((s16[2,144,256]{2,1,0:T(8,128)(2,1)S(1)}, s16[2,144,256]{2,1,0:T(8,128)(2,1)S(1)}, u32[]{:S(2)}, u32[]{:S(2)}) %collective-permute-start.7) | collective-permute-done | bytes 147488 | tf_op jit(solution)/shard_map/ppermute | solution.py:172
  129.7 0.0 copy-done
  129.7 0.8 shard_map.76
  (1 shorter events, 0.0 us)
Async XLA Ops:
  0.0 105.1 %copy-start.3 = (s32[1,1,1,32]{3,2,1,0:T(1,128)S(1)}, s32[1,1,1,32]{3,2,1,0:T(1,128)}, u32[]{:S(2)}) copy-start(s32[1,1,1,32]{3,2,1,0:T(1,128)} %param.9) | copy-start | bytes 388
  0.0 2.8 %collective-permute-start = (bf16[16,128,128]{2,1,0:T(8,128)(2,1)}, bf16[16,128,128]{2,1,0:T(8,128)(2,1)S(1)}, u32[]{:S(2)}, u32[]{:S(2)}) collective-permute-start(bf16[16,128,128]{2,1,0:T(8,128)(2,1)} %param.8), channel_id=1, source_target_pairs={{9,1},{11,3},{13,5},{15,7},{17,9},{19,11},{21,13},{23,15},{25,17},... | collective-permute-start | bytes 1572872 | tf_op jit(solution)/shard_map/ppermute | solution.py:151
  2.9 100.1 %collective-permute-start.1 = (bf16[32,128,128]{2,1,0:T(8,128)(2,1)S(1)}, bf16[32,128,128]{2,1,0:T(8,128)(2,1)S(1)}, u32[]{:S(2)}, u32[]{:S(2)}) collective-permute-start(bf16[32,128,128]{2,1,0:T(8,128)(2,1)S(1)} %constant_dynamic-update-slice_fusion.near), channel_id=1, source_target_pairs={{17,1},{19,3},{21,5},{23,7},{25,9},{27,11},{29,13},{31,15},{1,17},... | collective-permute-start | bytes 3145736 | tf_op jit(solution)/shard_map/ppermute | solution.py:153
  3.7 99.4 %collective-permute-start.2 = (bf16[16,128,128]{2,1,0:T(8,128)(2,1)S(1)}, bf16[16,128,128]{2,1,0:T(8,128)(2,1)S(1)}, u32[]{:S(2)}, u32[]{:S(2)}) collective-permute-start(bf16[16,128,128]{2,1,0:T(8,128)(2,1)S(1)} %collective-permute-done), channel_id=1, source_target_pairs={{1,0},{3,2},{5,4},{7,6},{9,8},{11,10},{13,12},{15,14},{17,16},{19,... | collective-permute-start | bytes 1572872 | tf_op jit(solution)/shard_map/ppermute | solution.py:154
  103.0 4.7 %copy-start.1 = (s32[1,1,1,16,12]{3,2,4,1,0:T(1,128)S(1)}, s32[1,1,1,16,12]{3,2,4,1,0:T(1,128)}, u32[]{:S(2)}) copy-start(s32[1,1,1,16,12]{3,2,4,1,0:T(1,128)} %param.10) | copy-start | bytes 2308
  103.0 4.7 %copy-start.2 = (s32[1,1,1,16,12]{3,2,4,1,0:T(1,128)S(1)}, s32[1,1,1,16,12]{3,2,4,1,0:T(1,128)}, u32[]{:S(2)}) copy-start(s32[1,1,1,16,12]{3,2,4,1,0:T(1,128)} %param.11) | copy-start | bytes 2308
  103.0 4.7 %collective-permute-start.3 = (bf16[32,128,128]{2,1,0:T(8,128)(2,1)S(1)}, bf16[32,128,128]{2,1,0:T(8,128)(2,1)S(1)}, u32[]{:S(2)}, u32[]{:S(2)}) collective-permute-start(bf16[32,128,128]{2,1,0:T(8,128)(2,1)S(1)} %collective-permute-done.1.far), channel_id=1, source_target_pairs={{1,0},{3,2},{5,4},{7,6},{9,8},{11,10},{13,12},{15,14},{17,16},{19,... | collective-permute-start | bytes 3145736 | tf_op jit(solution)/shard_map/ppermute | solution.py:158
  109.6 20.1 %copy-start = (f32[2,128,256]{2,1,0:T(8,128)S(1)}, f32[2,128,256]{2,1,0:T(8,128)}, u32[]{:S(2)}) copy-start(f32[2,128,256]{2,1,0:T(8,128)} %denominators.1) | copy-start | bytes 786436
  109.7 4.7 %collective-permute-start.4 = (f32[8,128,256]{2,1,0:T(8,128)S(1)}, f32[8,128,256]{2,1,0:T(8,128)S(1)}, u32[]{:S(2)}, u32[]{:S(2)}) collective-permute-start(f32[8,128,256]{2,1,0:T(8,128)S(1)} %shard_map.74), channel_id=1, source_target_pairs={{0,1},{1,0},{2,3},{3,2},{4,5},{5,4},{6,7},{7,6},{8,9},{9,8},{10,11... | collective-permute-start | bytes 3145736 | tf_op jit(solution)/shard_map/ppermute | solution.py:165
  114.6 9.8 %collective-permute-start.5 = (s16[2,144,256]{2,1,0:T(8,128)(2,1)S(1)}, s16[2,144,256]{2,1,0:T(8,128)(2,1)S(1)}, u32[]{:S(2)}, u32[]{:S(2)}) collective-permute-start(s16[2,144,256]{2,1,0:T(8,128)(2,1)S(1)} %get-tuple-element.16), channel_id=1, source_target_pairs={{0,4},{1,5},{2,6},{3,7},{4,0},{5,1},{6,2},{7,3},{8,12},{9,13},{10,... | collective-permute-start | bytes 442376 | tf_op jit(solution)/shard_map/ppermute | solution.py:172
  117.9 7.6 %collective-permute-start.6 = (s16[2,144,256]{2,1,0:T(8,128)(2,1)S(1)}, s16[2,144,256]{2,1,0:T(8,128)(2,1)S(1)}, u32[]{:S(2)}, u32[]{:S(2)}) collective-permute-start(s16[2,144,256]{2,1,0:T(8,128)(2,1)S(1)} %get-tuple-element.17), channel_id=1, source_target_pairs={{0,2},{1,7},{2,4},{3,1},{4,6},{5,3},{6,0},{7,5},{8,10},{9,15},{10,... | collective-permute-start | bytes 442376 | tf_op jit(solution)/shard_map/ppermute | solution.py:172
  121.5 8.2 %collective-permute-start.7 = (s16[2,144,256]{2,1,0:T(8,128)(2,1)S(1)}, s16[2,144,256]{2,1,0:T(8,128)(2,1)S(1)}, u32[]{:S(2)}, u32[]{:S(2)}) collective-permute-start(s16[2,144,256]{2,1,0:T(8,128)(2,1)S(1)} %get-tuple-element.18), channel_id=1, source_target_pairs={{0,6},{1,3},{2,0},{3,5},{4,2},{5,7},{6,4},{7,1},{8,14},{9,11},{10,... | collective-permute-start | bytes 442376 | tf_op jit(solution)/shard_map/ppermute | solution.py:172
